TPU v7x, 256 devices: a whole 4x4x8 slice. The times are simulated.
256 devices in a mesh: rows: 256 (over y, z, x, core).
Axes of the slice: x: 4, y: 4, z: 8, core: 2. Of those that a mesh axis runs over, the one named last changes fastest.
Arguments:
- features: bfloat16 [131072, 4096], P('rows'), may hold values from -90 to 90
- sketch_matrix: bfloat16 [4096, 320], replicated, may hold values from -8 to 8
Outputs:
- whitened: float32 [131072, 320], P('rows')
All inputs are finite; a program needn't handle non-finite values.
Results may differ from a plain program's by a relative error of at most 0.0015.
The roundings to bfloat16 on the way count: a program that leaves them out, or rounds other values in their place, can miss the bound.
Values may be sent and summed in bfloat16 or wider, within the bound.
No kernel may reach another device: no remote copies, remote signals or barrier semaphores. Data moves between devices by JAX's collectives and lax.ppermute only.
A program may use at most 64 MiB of HBM per device.

v0:
```python
import math

import jax
import jax.numpy as jnp
from jax import lax
from jax.sharding import PartitionSpec as P


def gram(block):
    return jnp.einsum(
        "rk,rl->kl",
        block,
        block,
        precision=lax.Precision.HIGHEST,
        preferred_element_type=jnp.float32,
    )


def upper_inverse(matrix):
    lower = jnp.linalg.cholesky(matrix)
    identity = jnp.eye(matrix.shape[0], dtype=matrix.dtype)
    return lax.linalg.triangular_solve(lower, identity, left_side=True, lower=True).T


def coupling_inverse(matrix):
    upper_inv = upper_inverse(matrix)
    return jnp.dot(upper_inv, upper_inv.T, precision=lax.Precision.HIGHEST)


def body(features, sketch_matrix):
    rows_total = features.shape[0] * lax.axis_size("rows")
    sketch = jnp.dot(features, sketch_matrix, preferred_element_type=jnp.float32)
    gram_one = lax.psum(gram(sketch), "rows")
    basis = jnp.dot(sketch, upper_inverse(gram_one), precision=lax.Precision.HIGHEST).astype(
        jnp.bfloat16
    )
    partial_coeffs = jnp.einsum("rd,rl->dl", features, basis, preferred_element_type=jnp.float32)
    coeffs = lax.psum(partial_coeffs, "rows")
    coupling = gram(coeffs)
    projected = jnp.dot(features, coeffs.astype(jnp.bfloat16), preferred_element_type=jnp.float32)
    whitened = jnp.dot(projected, coupling_inverse(coupling), precision=lax.Precision.HIGHEST)
    return whitened * math.sqrt(rows_total)


def solution(mesh):
    return jax.shard_map(
        body,
        mesh=mesh,
        in_specs=(P("rows", None), P()),
        out_specs=P("rows", None),
        check_vma=False,
    )
```

profile of v0, /device:TPU:1, one launch (start us, length us, event | category | flops | bytes accessed | tf_op | source)
XLA Modules:
  0.0 789.2 jit_solution(13488634524073234719)
XLA Ops:
  8.3 3.7 fusion.56
  15.1 253.1 %all-reduce.6.cloned.1.call-done = f32[320,320]{0,1:T(8,128)} async-done(((f32[320,320]{0,1:T(8,128)}), f32[320,320]{0,1:T(8,128)}) %all-reduce.6.cloned.1.call-update) | async-done | bytes 409616 | tf_op jit(solution)/shard_map/psum | solution.py:33
  272.2 11.7 %cholesky.214 = f32[128,128]{1,0:T(8,128)S(1)} custom-call(f32[128,128]{1,0:T(8,128)S(1)} %cholesky.324), custom_call_target="Cholesky" | custom-call | tf_op jit(solution)/shard_map/jit(cholesky)/cholesky | solution.py:20
  284.0 9.8 %custom-call.20 = f32[1,128,128]{1,2,0:T(8,128)S(1)} custom-call(f32[1,128,128]{2,1,0:T(8,128)S(1)} %get-tuple-element.52), custom_call_target="InvertDiagBlocksLowerTriangular" | custom-call | tf_op jit(solution)/shard_map/jit(cholesky)/cholesky | solution.py:20
  298.2 12.5 %cholesky.233 = f32[128,128]{1,0:T(8,128)S(1)} custom-call(f32[128,128]{1,0:T(8,128)} %cholesky.328), custom_call_target="Cholesky" | custom-call | tf_op jit(solution)/shard_map/jit(cholesky)/cholesky | solution.py:20
  311.4 11.0 %custom-call.21 = f32[1,128,128]{1,2,0:T(8,128)S(1)} custom-call(f32[1,128,128]{2,1,0:T(8,128)} %get-tuple-element.49), custom_call_target="InvertDiagBlocksLowerTriangular" | custom-call | tf_op jit(solution)/shard_map/jit(cholesky)/cholesky | solution.py:20
  324.4 5.8 cholesky.255
  335.8 5.7 while.4
  336.4 2.2 bitcast_dynamic-update-slice_fusion.4
  339.3 2.2 bitcast_dynamic-update-slice_fusion.4
  342.4 30.3 %custom-call.22 = f32[3,128,128]{1,2,0:T(8,128)S(1)} custom-call(f32[3,128,128]{2,1,0:T(8,128)} %pad_maximum_fusion), custom_call_target="InvertDiagBlocksLowerTriangular" | custom-call | tf_op jit(solution)/shard_map/triangular_solve/custom-call.2 | solution.py:22
  379.4 6.1 convolution_bitcast_fusion
  385.5 269.6 %all-reduce.8.cloned.1.call-done = f32[4096,320]{0,1:T(8,128)} async-done(((f32[4096,320]{0,1:T(8,128)}), f32[4096,320]{0,1:T(8,128)}) %all-reduce.8.cloned.1.call-update) | async-done | bytes 5242896 | tf_op jit(solution)/shard_map/psum | solution.py:38
  655.1 11.5 %fusion.58 = f32[320,320]{1,0:T(8,128)S(1)} fusion(f32[4096,320]{0,1:T(8,128)} %all-reduce.8.cloned.1.call-done), kind=kOutput, calls=%fused_computation.120 | convolution fusion | flops 5033164800 | bytes 5652480 | tf_op jit(solution)/shard_map/rk,rl->kl/dot_general | solution.py:10
  669.5 11.7 %cholesky.271 = f32[128,128]{1,0:T(8,128)S(1)} custom-call(f32[128,128]{1,0:T(8,128)S(1)} %cholesky.332), custom_call_target="Cholesky" | custom-call | tf_op jit(solution)/shard_map/jit(cholesky)/cholesky | solution.py:20
  682.1 9.8 %custom-call.23 = f32[1,128,128]{1,2,0:T(8,128)S(1)} custom-call(f32[1,128,128]{2,1,0:T(8,128)S(1)} %get-tuple-element.47), custom_call_target="InvertDiagBlocksLowerTriangular" | custom-call | tf_op jit(solution)/shard_map/jit(cholesky)/cholesky | solution.py:20
  694.9 11.7 %cholesky.290 = f32[128,128]{1,0:T(8,128)S(1)} custom-call(f32[128,128]{1,0:T(8,128)S(1)} %cholesky.336), custom_call_target="Cholesky" | custom-call | tf_op jit(solution)/shard_map/jit(cholesky)/cholesky | solution.py:20
  708.6 10.0 %custom-call.24 = f32[1,128,128]{1,2,0:T(8,128)S(1)} custom-call(f32[1,128,128]{2,1,0:T(8,128)S(1)} %get-tuple-element.44), custom_call_target="InvertDiagBlocksLowerTriangular" | custom-call | tf_op jit(solution)/shard_map/jit(cholesky)/cholesky | solution.py:20
  720.5 5.8 cholesky.312
  731.4 5.7 while.5
  732.0 2.2 bitcast_dynamic-update-slice_fusion.5
  734.8 2.2 bitcast_dynamic-update-slice_fusion.5
  737.2 30.1 %custom-call.25 = f32[3,128,128]{1,2,0:T(8,128)} custom-call(f32[3,128,128]{2,1,0:T(8,128)S(1)} %pad_maximum_fusion.1), custom_call_target="InvertDiagBlocksLowerTriangular" | custom-call | tf_op jit(solution)/shard_map/triangular_solve/custom-call.2 | solution.py:22
  774.7 5.3 fusion
  (82 shorter events, 52.8 us)
Async XLA Ops:
  6.5 1.7 copy-start
  6.5 261.6 %all-reduce.6.cloned.1.call-start = ((), (), s32[]{:S(2)}) async-start(), calls=%async_computation | async-start | bytes 983040 | tf_op jit(solution)/shard_map/psum | solution.py:33
  14.0 641.1 %all-reduce.8.cloned.1.call-start = ((), (), s32[]{:S(2)}) async-start(), calls=%async_computation.1 | async-start | bytes 10485760 | tf_op jit(solution)/shard_map/psum | solution.py:38
  271.4 0.8 copy-start.5
  335.1 0.8 copy-start.3
  668.7 0.8 copy-start.4
  669.5 97.8 %copy-start.1 = (f32[320,320]{1,0:T(8,128)S(1)}, f32[320,320]{1,0:T(8,128)}, u32[]{:S(2)}) copy-start(f32[320,320]{1,0:T(8,128)} %fusion.15) | copy-start | bytes 1228804
  730.6 0.8 copy-start.2
Sparse Core Ops, SparseCore 0:
  14.1 253.9 all-reduce.5
  385.6 269.4 all-reduce.7
where the time goes:
time: 794 us; the launch traced here: 789 us
  waiting for transfers between devices  523 us (66%)
  other arithmetic  173 us (22%)
  matrix products  54.4 us (7%)
  local copies, waits for them, and re-layouts  21.5 us (3%)
  between operations  17.7 us (2%)
    psum x1, waiting for transfers between devices, body(): coeffs = lax.psum(partial_coeffs, 'rows')  270 us
    psum x1, waiting for transfers between devices, body(): gram_one = lax.psum(gram(sketch), 'rows')  253 us
    another operation x21, other arithmetic, upper_inverse(): lower = jnp.linalg.cholesky(matrix)  106 us
    another operation x11, other arithmetic, upper_inverse(): lax.linalg.triangular_solve(lower, identity, left_side=True, lower=True)  63.5 us
  transfers between devices with their start and end apart: 2, of which 2 were waited for; matrix products, arithmetic and copies ran while one was open for 0% of the time, Pallas kernels for 0%

commit v1 on v0

v1 whole, which is shorter than its diff:
```python
import functools
import math

import jax
import jax.numpy as jnp
from jax import lax
from jax.experimental import pallas as pl
from jax.experimental.pallas import tpu as pltpu
from jax.sharding import PartitionSpec as P

SKETCH = 320
PAD = 384
BLOCK = 64
LANES = 128
WIDTH = 4 * LANES
F32 = jnp.float32
BF16 = jnp.bfloat16
HIGHEST = lax.Precision.HIGHEST

FIRST_AXIS = ("x", "y")
SECOND_AXIS = ("y", "x")
STREAM_BITS = ((0, 1), (1, 0))


def coordinates(index):
    return {"c": index & 1, "x": (index >> 1) & 3, "z": (index >> 3) & 7, "y": (index >> 6) & 3}


def device_at(place):
    return ((place["y"] * 8 + place["z"]) * 4 + place["x"]) * 2 + place["c"]


def gray(value):
    return value ^ (value >> 1)


def across(block):
    return lax.ppermute(block, "rows", [(i, i ^ 1) for i in range(lax.axis_size("rows"))])


def exchange(block, stream, step):
    pairs = []
    for i in range(lax.axis_size("rows")):
        place = coordinates(i)
        axis = FIRST_AXIS[place["c"]]
        wanted = gray(place[axis]) ^ (1 << STREAM_BITS[stream][step])
        place[axis] = next(v for v in range(4) if gray(v) == wanted)
        pairs.append((i, device_at(place)))
    return lax.ppermute(block, "rows", pairs)


def all_to_all(block, axes):
    size = block.shape[0]
    groups = []
    for i in range(lax.axis_size("rows")):
        place = coordinates(i)
        axis = axes[place["c"]]
        if place[axis] == 0:
            groups.append([device_at({**place, axis: k}) for k in range(size)])
    return lax.all_to_all(block, "rows", 0, 0, axis_index_groups=groups, tiled=True)


def scatter_sum(block, axes):
    return jnp.sum(all_to_all(block, axes), axis=0)


def gather(block, axes, size):
    return all_to_all(jnp.broadcast_to(block[None], (size, *block.shape)), axes)


def order(place, half, stream):
    core = place["c"] ^ half
    code = jnp.where(core == 0, *(gray(place[axis]) for axis in FIRST_AXIS))
    first, second = STREAM_BITS[stream]
    return core, (((code >> first) & 1) << 2) | (((code >> second) & 1) << 1)


def cross_blocks(id_ref, features, sketches, outs):
    place = coordinates(id_ref[0])
    for (half, stream, start), out in outs:
        core, mask = order(place, half, stream)
        for pair in range(out.shape[0] // 2):
            there = (core << 4) | (stream << 3) | ((start + 2 * pair) ^ mask)
            columns = features[:, pl.ds(pl.multiple_of(there * LANES, 256), 256)]
            both = jnp.dot(sketches[...], columns, preferred_element_type=F32)
            cross = both[:SKETCH] + both[SKETCH:]
            out[2 * pair] = cross[:, :LANES]
            out[2 * pair + 1] = cross[:, LANES:]


def send_kernel(id_ref, features_hbm, matrix_hbm, sketches, send0, send1, features, matrix, sems):
    chunks = sems.shape[1]
    width = features.shape[1] // chunks
    copies = []
    for n in range(chunks):
        columns = slice(n * width, (n + 1) * width)
        pair = [
            pltpu.make_async_copy(source.at[:, columns], target.at[:, columns], sems.at[m, n])
            for m, (source, target) in enumerate(((matrix_hbm, matrix), (features_hbm, features)))
        ]
        for copy in pair:
            copy.start()
        copies.append((columns, pair))
    sketch_t = jnp.zeros((SKETCH, features.shape[0]), F32)
    for columns, pair in copies:
        for copy in pair:
            copy.wait()
        sketch_t += dot_nt(matrix[:, columns], features[:, columns])
    high, low = split(sketch_t, 2)
    sketches[:SKETCH, :] = high
    sketches[SKETCH:, :] = low
    cross_blocks(id_ref, features, sketches, (((1, 0, 0), send0), ((1, 1, 0), send1)))


def keep_kernel(id_ref, features, sketches, low0, high0, low1, high1):
    wanted = ((0, 0, 0), (0, 0, 4), (0, 1, 0), (0, 1, 4))
    cross_blocks(id_ref, features, sketches, tuple(zip(wanted, (low0, high0, low1, high1))))


def call(kernel, operands, outs, scratch=(), flops=0, limit=24, space=pltpu.VMEM):
    vmem = pl.BlockSpec(memory_space=pltpu.VMEM)
    return pl.pallas_call(
        kernel,
        out_shape=[jax.ShapeDtypeStruct(shape, dtype) for shape, dtype in outs],
        in_specs=[pl.BlockSpec(memory_space=pltpu.SMEM)]
        + [pl.BlockSpec(memory_space=space)] * (len(operands) - 1),
        out_specs=[vmem] * len(outs),
        scratch_shapes=scratch,
        compiler_params=pltpu.CompilerParams(vmem_limit_bytes=limit * 1024 * 1024),
        cost_estimate=pl.CostEstimate(flops=flops, bytes_accessed=4 * 1024 * 1024, transcendentals=0),
    )(*operands)


def scatter_stream(stream, low, high, received):
    back = exchange(high + received[4:], stream, 0)
    block = low + received[:4]
    back_next = exchange(block[2:] + back[2:], stream, 1)
    return block[:2] + back[:2] + back_next


def split(value, terms):
    parts = []
    for _ in range(terms):
        part = value.astype(BF16)
        parts.append(part)
        value = value - part.astype(F32)
    return parts


def dot_nt(a, b, precision=None):
    return lax.dot_general(
        a, b, (((1,), (1,)), ((), ())), precision=precision, preferred_element_type=F32
    )


def dot(a, b, precision=None):
    return jnp.dot(a, b, precision=precision, preferred_element_type=F32)


def dot_three(a, b):
    a0, a1 = split(a, 2)
    b0, b1 = split(b, 2)
    return dot(a0, b0) + (dot(a0, b1) + dot(a1, b0))


def factor_blocks(blocks, outs):
    groups = BLOCK // 8
    lane = lax.broadcasted_iota(jnp.int32, (8, LANES), 1)
    sub = lax.broadcasted_iota(jnp.int32, (8, LANES), 0)
    work = []
    for block in blocks:
        rows = []
        for g in range(groups):
            unit = jnp.where(lane - BLOCK == sub + 8 * g, 1.0, 0.0).astype(F32)
            rows.append(jnp.where(lane < BLOCK, block[8 * g : 8 * g + 8], unit))
        work.append(rows)
    for g in range(groups):
        columns = [
            [
                [
                    jnp.broadcast_to(rows[r][:, 8 * g + j : 8 * g + j + 1], (8, LANES))
                    for r in range(g, groups)
                ]
                for j in range(8)
            ]
            for rows in work
        ]
        for k in range(8):
            for rows, cols, out in zip(work, columns, outs):
                pivot = cols[k][0][k : k + 1, :]
                inverse = 1.0 / pivot
                row = rows[g][k : k + 1, :]
                out[8 * g + k : 8 * g + k + 1, :] = row * lax.rsqrt(pivot)
                scaled = row * inverse
                for j in range(k + 1, 8):
                    factor = cols[j][0][k : k + 1, :] * inverse
                    for r in range(groups - g):
                        cols[j][r] = cols[j][r] - cols[k][r] * factor
                for r in range(g, groups):
                    column = cols[k][r - g]
                    if r == g:
                        column = jnp.where(sub > k, column, 0.0)
                    rows[r] = rows[r] - column * scaled


def factor_all(mats, outs, upper):
    column = lax.broadcasted_iota(jnp.int32, (BLOCK, PAD), 1)
    row = lax.broadcasted_iota(jnp.int32, (BLOCK, PAD), 0)
    lane = lax.broadcasted_iota(jnp.int32, (BLOCK, LANES), 1)
    line = lax.broadcasted_iota(jnp.int32, (BLOCK, LANES), 0)
    steps = SKETCH // BLOCK
    for step in range(steps):
        here = slice(step * BLOCK, (step + 1) * BLOCK)
        window = slice(step // 2 * LANES, (step // 2 + 1) * LANES)
        odd = step % 2 == 1
        blocks = []
        for mat in mats:
            block = mat[here, window]
            blocks.append(pltpu.roll(block, BLOCK, 1) if odd else block)
        factor_blocks(blocks, outs)
        inside = (column >= step * BLOCK) & (column < (step + 1) * BLOCK)
        for n, (mat, out) in enumerate(zip(mats, outs)):
            both = out[...]
            inverse = pltpu.roll(both, BLOCK, 1)[:, :BLOCK]
            line_up = jnp.where(inside, jnp.where(column - step * BLOCK == row, 1.0, 0.0), mat[here, :])
            panel = dot(inverse, line_up, HIGHEST)
            mat[here, :] = panel
            if n == 0:
                upper[here, :] = jnp.where(column >= (step + 1) * BLOCK, panel, 0.0)
                corner = jnp.where((lane < BLOCK) & (lane >= line), both, 0.0)
                corner = pltpu.roll(corner, BLOCK, 1) if odd else corner
                upper[here, window] = upper[here, window] + corner
            if step < steps - 1:
                start = (step + 1) * BLOCK // LANES * LANES
                change = dot(jnp.transpose(panel[:, start:]), panel, HIGHEST)
                below = slice((step + 1) * BLOCK, SKETCH)
                skip = (step + 1) * BLOCK - start
                keep = lax.broadcasted_iota(jnp.int32, (SKETCH - (step + 1) * BLOCK, PAD), 1)
                keep = (keep < step * BLOCK) | (keep >= (step + 1) * BLOCK)
                mat[below, :] = (
                    jnp.where(keep, mat[below, :], 0.0)
                    - change[skip : skip + SKETCH - (step + 1) * BLOCK]
                )


def columns_of(place, half, part, stream):
    core, mask = order(place, half, stream)
    first = (core << 4) | (stream << 3) | ((4 * part) ^ (mask & 4))
    return pl.ds(pl.multiple_of(first * LANES, WIDTH), WIDTH)


def lay_out(place, members, pieces, cross):
    for n, ((half, part, stream), piece) in enumerate(zip(members, pieces)):
        if len(piece.shape) == 2:
            cross[:, n * WIDTH : (n + 1) * WIDTH] = piece[...]
            continue
        _, mask = order(place, half, stream)
        for slot in range(4):
            start = n * WIDTH + (slot ^ (mask & 2)) * LANES
            cross[:, pl.ds(pl.multiple_of(start, LANES), LANES)] = piece[slot]


def products(place, members, cross, sketch_matrix_t, gram, coupling, left, right, mix):
    a, b, c = split(cross[...], 3)
    for n, term in enumerate((a, b, c)):
        left[n * SKETCH : (n + 1) * SKETCH, :] = term
    right[:SKETCH, :] = a
    right[SKETCH:PAD, :] = jnp.zeros((PAD - SKETCH, a.shape[1]), BF16)
    for n, member in enumerate(members):
        right[PAD:, n * WIDTH : (n + 1) * WIDTH] = sketch_matrix_t[:, columns_of(place, *member)]
    both = dot_nt(left[...], right[...])
    terms = [both[n * SKETCH : (n + 1) * SKETCH] for n in range(3)]
    for ref in (gram, coupling, mix):
        ref[...] = jnp.zeros_like(ref)
    gram[:SKETCH, :SKETCH] = terms[0][:, PAD:] + (terms[1][:, PAD:] + terms[2][:, PAD:])
    mix[:SKETCH, :SKETCH] = terms[1][:, :SKETCH] + terms[2][:, :SKETCH]
    coupling[:SKETCH, :SKETCH] = terms[0][:, :SKETCH] + dot_nt(b, b)
    coupling[...] += mix[...] + jnp.transpose(mix[...])


def pieces_kernel(members, id_ref, sketch_matrix_t, *refs):
    pieces, (cross, *rest) = refs[: len(members)], refs[len(members) :]
    place = coordinates(id_ref[0])
    lay_out(place, members, pieces, cross)
    products(place, members, cross, sketch_matrix_t, *rest)


def factor_kernel(members, scale, id_ref, sketch_matrix_t, *refs):
    pieces, refs = refs[: len(members)], refs[len(members) :]
    sums, (cross, basis_map, inverse_c) = refs[:6], refs[6:9]
    gram, coupling, left, right, mix, upper, out0, out1, wide = refs[9:]
    place = coordinates(id_ref[0])
    lay_out(place, members, pieces, cross)
    products(place, members, cross, sketch_matrix_t, gram, coupling, left, right, mix)
    gram[...] += sums[0][...] + (sums[2][...] + sums[4][...])
    coupling[...] += sums[1][...] + (sums[3][...] + sums[5][...])
    upper[...] = jnp.zeros_like(upper)
    factor_all((gram, coupling), (out0, out1), upper)
    row = lax.broadcasted_iota(jnp.int32, (PAD, PAD), 0)
    column = lax.broadcasted_iota(jnp.int32, (PAD, PAD), 1)
    lower = (row < SKETCH) & (column <= row)
    high, low = split(jnp.where(lower, gram[...], 0.0)[:SKETCH, :SKETCH], 2)
    for n, term in enumerate((high, high, low)):
        wide[:, n * SKETCH : (n + 1) * SKETCH] = term.astype(F32)
    basis_map[...] = wide[...].astype(BF16)
    chain = dot_nt(jnp.where(lower, coupling[...], 0.0), upper[...], HIGHEST)
    mix[...] = dot(jnp.transpose(chain), chain, HIGHEST) * scale
    inverse_c[...] = mix[:SKETCH, :SKETCH]


def final_kernel(sets, id_ref, features, basis_map, inverse_c, *refs):
    crosses, (result, stack) = refs[:-2], refs[-2:]
    place = coordinates(id_ref[0])
    total = jnp.zeros(result.shape, F32)
    for cross, members in zip(crosses, sets):
        for n, member in enumerate(members):
            a, b = split(cross[:, n * WIDTH : (n + 1) * WIDTH], 2)
            for m, term in enumerate((a, b, a)):
                stack[m * SKETCH : (m + 1) * SKETCH, :] = term
            coeffs = dot(basis_map[...], stack[...])
            total += dot_nt(coeffs.astype(BF16), features[:, columns_of(place, *member)])
    result[...] = dot_three(inverse_c[...], total)


def body(features, sketch_matrix):
    rows, width = features.shape
    rows_total = rows * lax.axis_size("rows")
    device = lax.axis_index("rows").astype(jnp.int32)[None]
    whole, piece = ((8, SKETCH, LANES), F32), ((4, SKETCH, LANES), F32)
    flops = 2 * rows * width * SKETCH

    sketch_matrix_t = sketch_matrix.T

    sketches, send0, send1 = call(
        send_kernel,
        (device, features, sketch_matrix_t),
        [((2 * SKETCH, rows), BF16), whole, whole],
        scratch=[
            pltpu.VMEM((rows, width), BF16),
            pltpu.VMEM((SKETCH, width), BF16),
            pltpu.SemaphoreType.DMA((2, 4)),
        ],
        flops=2 * flops,
        space=pltpu.HBM,
        limit=50,
    )
    received = across(send0), across(send1)
    low0, high0, low1, high1 = call(
        keep_kernel, (device, features, sketches), [piece] * 4, flops=flops
    )
    block = jnp.concatenate(
        [scatter_stream(0, low0, high0, received[0]), scatter_stream(1, low1, high1, received[1])]
    )
    block = scatter_sum(block, SECOND_AXIS)
    block = scatter_sum(block.reshape(8, SKETCH // 8, LANES), ("z", "z"))
    block = gather(block, ("z", "z"), 8).reshape(SKETCH, LANES)
    block = gather(block, SECOND_AXIS, 4)
    first, second = [], []
    for stream in range(2):
        own = block[2 * stream : 2 * stream + 2]
        own = jnp.concatenate([own, exchange(own, stream, 1)])
        first.append(own)
        second.append(exchange(own, stream, 0))

    sets = [
        ((0, 0, 0),),
        ((0, 0, 1), (0, 1, 0), (0, 1, 1)),
        ((1, 0, 0), (1, 0, 1)),
        ((1, 1, 0), (1, 1, 1)),
    ]
    square = ((PAD, PAD), F32)

    def scratch_for(members):
        width = len(members) * WIDTH
        return [
            pltpu.VMEM((3 * SKETCH, width), BF16),
            pltpu.VMEM((PAD + SKETCH, width), BF16),
            pltpu.VMEM(*square),
        ]

    def cross_shape(members):
        return ((SKETCH, len(members) * WIDTH), F32)

    def sums_of(members, pieces):
        return call(
            functools.partial(pieces_kernel, members),
            (device, sketch_matrix_t, *pieces),
            [cross_shape(members), square, square],
            scratch=scratch_for(members),
        )

    cross0, *sums0 = sums_of(sets[0], first[:1])
    other = [across(block) for block in (cross0, first[1], *second)]
    cross1, *sums1 = sums_of(sets[1], [first[1], *second])
    cross2, *sums2 = sums_of(sets[2], other[:2])
    corner = pltpu.VMEM((BLOCK, LANES), F32)
    cross3, basis_map, inverse_c = call(
        functools.partial(factor_kernel, sets[3], math.sqrt(rows_total)),
        (device, sketch_matrix_t, *other[2:], *sums0, *sums1, *sums2),
        [cross_shape(sets[3]), ((SKETCH, 3 * SKETCH), BF16), ((SKETCH, SKETCH), F32)],
        scratch=[pltpu.VMEM(*square)] * 2
        + scratch_for(sets[3])
        + [pltpu.VMEM(*square), corner, corner, pltpu.VMEM((SKETCH, 3 * SKETCH), F32)],
        flops=flops,
    )
    (result,) = call(
        functools.partial(final_kernel, sets),
        (device, features, basis_map, inverse_c, cross0, cross1, cross2, cross3),
        [((SKETCH, rows), F32)],
        scratch=[pltpu.VMEM((3 * SKETCH, WIDTH), BF16)],
        flops=4 * flops,
    )
    return result.T


def solution(mesh):
    return jax.shard_map(
        body,
        mesh=mesh,
        in_specs=(P("rows", None), P()),
        out_specs=P("rows", None),
        check_vma=False,
    )
```

time: 794 us -> 141 us (0.18)
  waiting for transfers between devices: 523 us -> 25.9 us
  other arithmetic: 173 us -> 0.71 us
  matrix products: 54.4 us -> 0 us
  blocking collectives: 0 us -> 47.3 us
  Pallas kernels: 0 us -> 39.1 us
  starting transfers between devices: 0.22 us -> 27.6 us
  local copies, waits for them, and re-layouts: 21.5 us -> 0.11 us
  between operations: 17.7 us -> 0.2 us
    psum x2 -> x0, waiting for transfers between devices: 523 us -> none  [the longest x1 270 us: body(): coeffs = lax.psum(partial_coeffs, 'rows')]
    another operation x32 -> x0, other arithmetic: 169 us -> none  [the longest x21 106 us: upper_inverse(): lower = jnp.linalg.cholesky(matrix)]
    all_to_all x0 -> x4, blocking collectives: none -> 47.3 us  [all_to_all(): lax.all_to_all(block, 'rows', 0, 0, axis_index_groups=groups, tiled=True)]
    pallas_call x0 -> x7, Pallas kernels: none -> 39.1 us  [call(): pl.pallas_call(kernel, out_shape=[jax.ShapeDtypeStruct(shape, dtype) for...]
    dot_general x8 -> x0, matrix products: 33.5 us -> none  [the longest x2 13.5 us: gram(): jnp.einsum('rk,rl->kl', block, block, precision=lax.Precision.HIGHEST, pr...]
    ppermute x0 -> x14, starting transfers between devices: none -> 27.6 us  [the longest x6 22.2 us: across(): lax.ppermute(block, 'rows', [(i, i ^ 1) for i in range(lax.axis_size('row...]
    ppermute x0 -> x14, waiting for transfers between devices: none -> 25.9 us  [the longest x8 24.2 us: exchange(): return lax.ppermute(block, 'rows', pairs)]
    another operation x18 -> x0, matrix products: 20.9 us -> none  [the longest x10 11.2 us: upper_inverse(): lax.linalg.triangular_solve(lower, identity, left_side=True, lower=True)]
  transfers between devices with their start and end apart: 2 -> 14, of which waited for: 2 -> 7; matrix products, arithmetic and copies ran while one was open for 0% -> 0% of each run, Pallas kernels for 0% -> 6%
where the time goes in v1:
time: 141 us
  blocking collectives  47.3 us (34%)
  Pallas kernels  39.1 us (28%)
  starting transfers between devices  27.6 us (20%)
  waiting for transfers between devices  25.9 us (18%)
    all_to_all x4, blocking collectives, all_to_all(): lax.all_to_all(block, 'rows', 0, 0, axis_index_groups=groups, tiled=True)  47.3 us
    pallas_call x7, Pallas kernels, call(): pl.pallas_call(kernel, out_shape=[jax.ShapeDtypeStruct(shape, dtype) for...  39.1 us
    ppermute x8, waiting for transfers between devices, exchange(): return lax.ppermute(block, 'rows', pairs)  24.2 us
    ppermute x6, starting transfers between devices, across(): lax.ppermute(block, 'rows', [(i, i ^ 1) for i in range(lax.axis_size('row...  22.2 us
    ppermute x8, starting transfers between devices, exchange(): return lax.ppermute(block, 'rows', pairs)  5.43 us
  transfers between devices with their start and end apart: 14, of which 7 were waited for; matrix products, arithmetic and copies ran while one was open for 0% of the time, Pallas kernels for 6%

profile of v1, /device:TPU:1, one launch (start us, length us, event | category | flops | bytes accessed | tf_op | source)
XLA Modules:
  0.0 140.9 jit_solution(2745524159167783889)
XLA Ops:
  0.0 5.3 %shard_map.28 = (bf16[640,512]{1,0:T(8,128)(2,1)S(1)}, f32[8,320,128]{2,1,0:T(8,128)S(1)}, f32[8,320,128]{2,1,0:T(8,128)S(1)}) custom-call(s32[1]{0:T(128)} %bitcast.id_ref, bf16[512,4096]{1,0:T(8,128)(2,1)} %features.3, bf16[320,4096]{1,0:T(8,128)(2,1)} %bitcast.5), custom_call_target="tpu_custom_call" | custom-call | flops 2684354560 | bytes 4194304 | tf_op jit(solution)/shard_map/pallas_call | solution.py:122
  5.3 3.3 %collective-permute-start.3 = (f32[8,320,128]{2,1,0:T(8,128)S(1)}, f32[8,320,128]{2,1,0:T(8,128)S(1)}, u32[]{:S(2)}, u32[]{:S(2)}) collective-permute-start(f32[8,320,128]{2,1,0:T(8,128)S(1)} %get-tuple-element.29), channel_id=1, source_target_pairs={{0,1},{1,0},{2,3},{3,2},{4,5},{5,4},{6,7},{7,6},{8,9},{9,8},{10,11... | collective-permute-start | bytes 3932168 | tf_op jit(solution)/shard_map/ppermute | solution.py:38
  8.8 1.5 %shard_map.29 = (f32[4,320,128]{2,1,0:T(8,128)S(1)}, f32[4,320,128]{2,1,0:T(8,128)S(1)}, f32[4,320,128]{2,1,0:T(8,128)S(1)}, f32[4,320,128]{2,1,0:T(8,128)S(1)}) custom-call(s32[1]{0:T(128)} %bitcast.id_ref, bf16[512,4096]{1,0:T(8,128)(2,1)S(1)} %copy-done.1, bf16[640,512]{1,0:T(8,128)(2,1)S(1)} %get-tuple-element.24.sketches), custom_call_target="tpu_custom_call" | custom-call | flops 1342177280 | bytes 4194304 | tf_op jit(solution)/shard_map/pallas_call | solution.py:122
  10.3 1.0 collective-permute-done.3
  11.4 1.1 collective-permute-start.4
  13.4 9.1 %collective-permute-done.4 = f32[4,320,128]{2,1,0:T(8,128)S(1)} collective-permute-done((f32[4,320,128]{2,1,0:T(8,128)S(1)}, f32[4,320,128]{2,1,0:T(8,128)S(1)}, u32[]{:S(2)}, u32[]{:S(2)}) %collective-permute-start.4) | collective-permute-done | bytes 655392 | tf_op jit(solution)/shard_map/ppermute | solution.py:49
  23.2 1.1 collective-permute-start.2
  24.3 4.5 %collective-permute-done.5 = f32[2,320,128]{2,1,0:T(8,128)S(1)} collective-permute-done((f32[2,320,128]{2,1,0:T(8,128)S(1)}, f32[2,320,128]{2,1,0:T(8,128)S(1)}, u32[]{:S(2)}, u32[]{:S(2)}) %collective-permute-start.5) | collective-permute-done | bytes 327712 | tf_op jit(solution)/shard_map/ppermute | solution.py:49
  28.9 1.8 %collective-permute-done.2 = f32[2,320,128]{2,1,0:T(8,128)S(1)} collective-permute-done((f32[2,320,128]{2,1,0:T(8,128)S(1)}, f32[2,320,128]{2,1,0:T(8,128)S(1)}, u32[]{:S(2)}, u32[]{:S(2)}) %collective-permute-start.2) | collective-permute-done | bytes 327712 | tf_op jit(solution)/shard_map/ppermute | solution.py:49
  30.8 10.5 %all_to_all.20 = f32[4,320,128]{2,1,0:T(8,128)S(1)} all-to-all(f32[4,320,128]{2,1,0:T(8,128)S(1)} %pad_maximum_fusion), channel_id=1, replica_groups={{0,64,128,192},{1,3,5,7},{2,66,130,194},{4,68,132,196},{6,70,134,198},{..., dimensions={0} | all-to-all | bytes 1310720 | tf_op jit(solution)/shard_map/all_to_all | solution.py:60
  41.4 16.0 %all_to_all.21 = f32[8,40,128]{2,1,0:T(8,128)S(1)} all-to-all(f32[8,40,128]{2,1,0:T(8,128)S(1)} %bitcast.10), channel_id=1, replica_groups={{0,8,16,24,32,40,48,56},{1,9,17,25,33,41,49,57},{2,10,18,26,34,42,50,58..., dimensions={0} | all-to-all | bytes 327680 | tf_op jit(solution)/shard_map/all_to_all | solution.py:60
  57.5 10.7 %all_to_all.22 = f32[8,40,128]{2,1,0:T(8,128)S(1)} all-to-all(f32[8,40,128]{2,1,0:T(8,128)S(1)} %broadcast_in_dim.17), channel_id=1, replica_groups={{0,8,16,24,32,40,48,56},{1,9,17,25,33,41,49,57},{2,10,18,26,34,42,50,58..., dimensions={0} | all-to-all | bytes 327680 | tf_op jit(solution)/shard_map/all_to_all | solution.py:60
  68.2 10.0 %all_to_all.23 = f32[4,320,128]{2,1,0:T(8,128)S(1)} all-to-all(f32[4,320,128]{2,1,0:T(8,128)S(1)} %broadcast_in_dim.19), channel_id=1, replica_groups={{0,64,128,192},{1,3,5,7},{2,66,130,194},{4,68,132,196},{6,70,134,198},{..., dimensions={0} | all-to-all | bytes 1310720 | tf_op jit(solution)/shard_map/all_to_all | solution.py:60
  78.3 2.1 %collective-permute-start.6 = (f32[2,320,128]{2,1,0:T(8,128)S(1)}, f32[2,320,128]{2,1,0:T(8,128)S(1)}, u32[]{:S(2)}, u32[]{:S(2)}) collective-permute-start(f32[2,320,128]{2,1,0:T(8,128)S(1)} %get-tuple-element.48), channel_id=1, source_target_pairs={{0,6},{1,193},{2,4},{3,195},{4,2},{5,197},{6,0},{7,199},{8,14},{9,... | collective-permute-start | bytes 983048 | tf_op jit(solution)/shard_map/ppermute | solution.py:49
  80.4 8.3 %collective-permute-done.6 = f32[2,320,128]{2,1,0:T(8,128)S(1)} collective-permute-done((f32[2,320,128]{2,1,0:T(8,128)S(1)}, f32[2,320,128]{2,1,0:T(8,128)S(1)}, u32[]{:S(2)}, u32[]{:S(2)}) %collective-permute-start.6) | collective-permute-done | bytes 327712 | tf_op jit(solution)/shard_map/ppermute | solution.py:49
  88.9 0.8 collective-permute-start.10
  89.8 9.6 %collective-permute-start.13 = (f32[4,320,128]{2,1,0:T(8,128)S(1)}, f32[4,320,128]{2,1,0:T(8,128)S(1)}, u32[]{:S(2)}, u32[]{:S(2)}) collective-permute-start(f32[4,320,128]{2,1,0:T(8,128)S(1)} %pad_maximum_fusion.2.refs_0_), channel_id=1, source_target_pairs={{0,1},{1,0},{2,3},{3,2},{4,5},{5,4},{6,7},{7,6},{8,9},{9,8},{10,11... | collective-permute-start | bytes 1966088 | tf_op jit(solution)/shard_map/ppermute | solution.py:38
  99.4 1.3 shard_map.30
  101.0 6.7 %collective-permute-start.8 = (f32[4,320,128]{2,1,0:T(8,128)S(1)}, f32[4,320,128]{2,1,0:T(8,128)S(1)}, u32[]{:S(2)}, u32[]{:S(2)}) collective-permute-start(f32[4,320,128]{2,1,0:T(8,128)S(1)} %collective-permute-done.7.refs_1_), channel_id=1, source_target_pairs={{0,1},{1,0},{2,3},{3,2},{4,5},{5,4},{6,7},{7,6},{8,9},{9,8},{10,11... | collective-permute-start | bytes 1966088 | tf_op jit(solution)/shard_map/ppermute | solution.py:38
  107.7 2.2 %collective-permute-start.11 = (f32[4,320,128]{2,1,0:T(8,128)S(1)}, f32[4,320,128]{2,1,0:T(8,128)S(1)}, u32[]{:S(2)}, u32[]{:S(2)}) collective-permute-start(f32[4,320,128]{2,1,0:T(8,128)S(1)} %collective-permute-done.10.refs_2_), channel_id=1, source_target_pairs={{0,1},{1,0},{2,3},{3,2},{4,5},{5,4},{6,7},{7,6},{8,9},{9,8},{10,11... | collective-permute-start | bytes 1966088 | tf_op jit(solution)/shard_map/ppermute | solution.py:38
  109.8 3.3 %shard_map.31 = (f32[320,1536]{1,0:T(8,128)S(1)}, f32[384,384]{1,0:T(8,128)S(1)}, f32[384,384]{1,0:T(8,128)S(1)}) custom-call(s32[1]{0:T(128)} %bitcast.id_ref, bf16[320,4096]{1,0:T(8,128)(2,1)S(1)} %bitcast.7, f32[4,320,128]{2,1,0:T(8,128)S(1)} %pad_maximum_fusion.2.refs_0_, f32[4,320,128]{2,1,0:T(8,128)S(1)} %collective-permute-done.7.refs_1_, ...), custom_call_target="tpu_custom_call" | custom-call | bytes 4194304 | tf_op jit(solution)/shard_map/pallas_call | solution.py:122
  113.2 2.3 %shard_map.32 = (f32[320,1024]{1,0:T(8,128)S(1)}, f32[384,384]{1,0:T(8,128)S(1)}, f32[384,384]{1,0:T(8,128)S(1)}) custom-call(s32[1]{0:T(128)} %bitcast.id_ref, bf16[320,4096]{1,0:T(8,128)(2,1)S(1)} %bitcast.8, f32[320,512]{1,0:T(8,128)S(1)} %collective-permute-done.12.refs_0_, f32[4,320,128]{2,1,0:T(8,128)S(1)} %collective-permute-done.13.refs_1_), custom_call_target="tpu_custom_call" | custom-call | bytes 4194304 | tf_op jit(solution)/shard_map/pallas_call | solution.py:122
  115.5 19.0 %shard_map.33 = (f32[320,1024]{1,0:T(8,128)S(1)}, bf16[320,960]{1,0:T(8,128)(2,1)S(1)}, f32[320,320]{1,0:T(8,128)S(1)}) custom-call(s32[1]{0:T(128)} %bitcast.id_ref, bf16[320,4096]{1,0:T(8,128)(2,1)S(1)} %bitcast.9, f32[4,320,128]{2,1,0:T(8,128)S(1)} %collective-permute-done.8.refs_0_, f32[4,320,128]{2,1,0:T(8,128)S(1)} %collective-permute-done.11.refs_1_, ...), custom_call_target="tpu_custom_call" | custom-call | flops 1342177280 | bytes 4194304 | tf_op jit(solution)/shard_map/pallas_call | solution.py:122
  134.6 6.3 %shard_map.34 = f32[320,512]{1,0:T(8,128)} custom-call(s32[1]{0:T(128)} %bitcast.id_ref, bf16[512,4096]{1,0:T(8,128)(2,1)S(1)} %copy-done.2, bf16[320,960]{1,0:T(8,128)(2,1)S(1)} %get-tuple-element.38.basis_map, f32[320,320]{1,0:T(8,128)S(1)} %get-tuple-element.39.inverse_c, f32[320,512]{1,0:T(8,128)S(1)} %get-tuple-element.35.refs_0_, ...), custom_call_target="tpu_custom_call" | custom-call | flops 5368709120 | bytes 4194304 | tf_op jit(solution)/shard_map/pallas_call | solution.py:122
  (35 shorter events, 2.7 us)
Async XLA Ops:
  0.0 8.8 %copy-start.1 = (bf16[512,4096]{1,0:T(8,128)(2,1)S(1)}, bf16[512,4096]{1,0:T(8,128)(2,1)}, u32[]{:S(2)}) copy-start(bf16[512,4096]{1,0:T(8,128)(2,1)} %features.3) | copy-start | bytes 12582916
  5.3 6.0 %collective-permute-start.3 = (f32[8,320,128]{2,1,0:T(8,128)S(1)}, f32[8,320,128]{2,1,0:T(8,128)S(1)}, u32[]{:S(2)}, u32[]{:S(2)}) collective-permute-start(f32[8,320,128]{2,1,0:T(8,128)S(1)} %get-tuple-element.29), channel_id=1, source_target_pairs={{0,1},{1,0},{2,3},{3,2},{4,5},{5,4},{6,7},{7,6},{8,9},{9,8},{10,11... | collective-permute-start | bytes 3932168 | tf_op jit(solution)/shard_map/ppermute | solution.py:38
  8.7 4.5 %collective-permute-start = (f32[8,320,128]{2,1,0:T(8,128)S(1)}, f32[8,320,128]{2,1,0:T(8,128)S(1)}, u32[]{:S(2)}, u32[]{:S(2)}) collective-permute-start(f32[8,320,128]{2,1,0:T(8,128)S(1)} %get-tuple-element.26), channel_id=1, source_target_pairs={{0,1},{1,0},{2,3},{3,2},{4,5},{5,4},{6,7},{7,6},{8,9},{9,8},{10,11... | collective-permute-start | bytes 3932168 | tf_op jit(solution)/shard_map/ppermute | solution.py:38
  11.4 11.0 %collective-permute-start.4 = (f32[4,320,128]{2,1,0:T(8,128)S(1)}, f32[4,320,128]{2,1,0:T(8,128)S(1)}, u32[]{:S(2)}, u32[]{:S(2)}) collective-permute-start(f32[4,320,128]{2,1,0:T(8,128)S(1)} %get-tuple-element.46), channel_id=1, source_target_pairs={{0,6},{1,193},{2,4},{3,195},{4,2},{5,197},{6,0},{7,199},{8,14},{9,... | collective-permute-start | bytes 1966088 | tf_op jit(solution)/shard_map/ppermute | solution.py:49
  13.3 9.8 %collective-permute-start.1 = (f32[4,320,128]{2,1,0:T(8,128)S(1)}, f32[4,320,128]{2,1,0:T(8,128)S(1)}, u32[]{:S(2)}, u32[]{:S(2)}) collective-permute-start(f32[4,320,128]{2,1,0:T(8,128)S(1)} %get-tuple-element.44), channel_id=1, source_target_pairs={{0,2},{1,65},{2,0},{3,67},{4,6},{5,69},{6,4},{7,71},{8,10},{9,73},... | collective-permute-start | bytes 1966088 | tf_op jit(solution)/shard_map/ppermute | solution.py:49
  22.5 6.3 %collective-permute-start.5 = (f32[2,320,128]{2,1,0:T(8,128)S(1)}, f32[2,320,128]{2,1,0:T(8,128)S(1)}, u32[]{:S(2)}, u32[]{:S(2)}) collective-permute-start(f32[2,320,128]{2,1,0:T(8,128)S(1)} %slice_add_fusion.4), channel_id=1, source_target_pairs={{0,2},{1,65},{2,0},{3,67},{4,6},{5,69},{6,4},{7,71},{8,10},{9,73},... | collective-permute-start | bytes 983048 | tf_op jit(solution)/shard_map/ppermute | solution.py:49
  23.2 7.5 %collective-permute-start.2 = (f32[2,320,128]{2,1,0:T(8,128)S(1)}, f32[2,320,128]{2,1,0:T(8,128)S(1)}, u32[]{:S(2)}, u32[]{:S(2)}) collective-permute-start(f32[2,320,128]{2,1,0:T(8,128)S(1)} %slice_add_fusion.6), channel_id=1, source_target_pairs={{0,6},{1,193},{2,4},{3,195},{4,2},{5,197},{6,0},{7,199},{8,14},{9,... | collective-permute-start | bytes 983048 | tf_op jit(solution)/shard_map/ppermute | solution.py:49
  78.3 10.5 %collective-permute-start.6 = (f32[2,320,128]{2,1,0:T(8,128)S(1)}, f32[2,320,128]{2,1,0:T(8,128)S(1)}, u32[]{:S(2)}, u32[]{:S(2)}) collective-permute-start(f32[2,320,128]{2,1,0:T(8,128)S(1)} %get-tuple-element.48), channel_id=1, source_target_pairs={{0,6},{1,193},{2,4},{3,195},{4,2},{5,197},{6,0},{7,199},{8,14},{9,... | collective-permute-start | bytes 983048 | tf_op jit(solution)/shard_map/ppermute | solution.py:49
  80.4 19.0 %copy-start = (bf16[4096,320]{0,1:T(8,128)(2,1)S(1)}, bf16[4096,320]{0,1:T(8,128)(2,1)}, u32[]{:S(2)}) copy-start(bf16[4096,320]{0,1:T(8,128)(2,1)} %param.3) | copy-start | bytes 7864324
  80.4 8.5 %collective-permute-start.9 = (f32[2,320,128]{2,1,0:T(8,128)S(1)}, f32[2,320,128]{2,1,0:T(8,128)S(1)}, u32[]{:S(2)}, u32[]{:S(2)}) collective-permute-start(f32[2,320,128]{2,1,0:T(8,128)S(1)} %get-tuple-element.47), channel_id=1, source_target_pairs={{0,2},{1,65},{2,0},{3,67},{4,6},{5,69},{6,4},{7,71},{8,10},{9,73},... | collective-permute-start | bytes 983048 | tf_op jit(solution)/shard_map/ppermute | solution.py:49
  88.8 12.2 %collective-permute-start.7 = (f32[4,320,128]{2,1,0:T(8,128)S(1)}, f32[4,320,128]{2,1,0:T(8,128)S(1)}, u32[]{:S(2)}, u32[]{:S(2)}) collective-permute-start(f32[4,320,128]{2,1,0:T(8,128)S(1)} %pad_maximum_fusion.1.refs_0_), channel_id=1, source_target_pairs={{0,2},{1,65},{2,0},{3,67},{4,6},{5,69},{6,4},{7,71},{8,10},{9,73},... | collective-permute-start | bytes 1966088 | tf_op jit(solution)/shard_map/ppermute | solution.py:49
  88.9 18.7 %collective-permute-start.10 = (f32[4,320,128]{2,1,0:T(8,128)S(1)}, f32[4,320,128]{2,1,0:T(8,128)S(1)}, u32[]{:S(2)}, u32[]{:S(2)}) collective-permute-start(f32[4,320,128]{2,1,0:T(8,128)S(1)} %pad_maximum_fusion.2.refs_0_), channel_id=1, source_target_pairs={{0,6},{1,193},{2,4},{3,195},{4,2},{5,197},{6,0},{7,199},{8,14},{9,... | collective-permute-start | bytes 1966088 | tf_op jit(solution)/shard_map/ppermute | solution.py:49
  89.8 23.4 %collective-permute-start.13 = (f32[4,320,128]{2,1,0:T(8,128)S(1)}, f32[4,320,128]{2,1,0:T(8,128)S(1)}, u32[]{:S(2)}, u32[]{:S(2)}) collective-permute-start(f32[4,320,128]{2,1,0:T(8,128)S(1)} %pad_maximum_fusion.2.refs_0_), channel_id=1, source_target_pairs={{0,1},{1,0},{2,3},{3,2},{4,5},{5,4},{6,7},{7,6},{8,9},{9,8},{10,11... | collective-permute-start | bytes 1966088 | tf_op jit(solution)/shard_map/ppermute | solution.py:38
  100.7 12.5 %collective-permute-start.12 = (f32[320,512]{1,0:T(8,128)S(1)}, f32[320,512]{1,0:T(8,128)S(1)}, u32[]{:S(2)}, u32[]{:S(2)}) collective-permute-start(f32[320,512]{1,0:T(8,128)S(1)} %get-tuple-element.35.refs_0_), channel_id=1, source_target_pairs={{0,1},{1,0},{2,3},{3,2},{4,5},{5,4},{6,7},{7,6},{8,9},{9,8},{10,11... | collective-permute-start | bytes 1966088 | tf_op jit(solution)/shard_map/ppermute | solution.py:38
  101.0 14.5 %collective-permute-start.8 = (f32[4,320,128]{2,1,0:T(8,128)S(1)}, f32[4,320,128]{2,1,0:T(8,128)S(1)}, u32[]{:S(2)}, u32[]{:S(2)}) collective-permute-start(f32[4,320,128]{2,1,0:T(8,128)S(1)} %collective-permute-done.7.refs_1_), channel_id=1, source_target_pairs={{0,1},{1,0},{2,3},{3,2},{4,5},{5,4},{6,7},{7,6},{8,9},{9,8},{10,11... | collective-permute-start | bytes 1966088 | tf_op jit(solution)/shard_map/ppermute | solution.py:38
  107.7 7.8 %collective-permute-start.11 = (f32[4,320,128]{2,1,0:T(8,128)S(1)}, f32[4,320,128]{2,1,0:T(8,128)S(1)}, u32[]{:S(2)}, u32[]{:S(2)}) collective-permute-start(f32[4,320,128]{2,1,0:T(8,128)S(1)} %collective-permute-done.10.refs_2_), channel_id=1, source_target_pairs={{0,1},{1,0},{2,3},{3,2},{4,5},{5,4},{6,7},{7,6},{8,9},{9,8},{10,11... | collective-permute-start | bytes 1966088 | tf_op jit(solution)/shard_map/ppermute | solution.py:38
  115.5 19.0 %copy-start.2 = (bf16[512,4096]{1,0:T(8,128)(2,1)S(1)}, bf16[512,4096]{1,0:T(8,128)(2,1)}, u32[]{:S(2)}) copy-start(bf16[512,4096]{1,0:T(8,128)(2,1)} %features.3) | copy-start | bytes 12582916

commit v2 on v1

--- a/solution.py
+++ b/solution.py
@@ -15,10 +15,9 @@
 WIDTH = 4 * LANES
 F32 = jnp.float32
 BF16 = jnp.bfloat16
-HIGHEST = lax.Precision.HIGHEST
-
-FIRST_AXIS = ("x", "y")
-SECOND_AXIS = ("y", "x")
+
+FIRST_AXIS = ("y", "x")
+SECOND_AXIS = ("x", "y")
 STREAM_BITS = ((0, 1), (1, 0))
 
 
@@ -163,7 +162,25 @@
     return dot(a0, b0) + (dot(a0, b1) + dot(a1, b0))
 
 
-def factor_blocks(blocks, outs):
+def stacked(rows, terms):
+    parts = split(rows, 3)
+    return jnp.concatenate([parts[n] for n in terms], axis=0)
+
+
+def beside(value):
+    lane = lax.broadcasted_iota(jnp.int32, value.shape, 1)
+    parts = [part.astype(F32) for part in split(value, 3)]
+    turned = [pltpu.roll(part, BLOCK, 1) for part in parts[:2]]
+    pairs = ((0, 0), (1, 0), (2, 1))
+    return jnp.concatenate(
+        [jnp.where(lane < BLOCK, parts[m], turned[n]).astype(BF16) for m, n in pairs], axis=1
+    )
+
+
+UNDER = (0, 1, 0, 2, 0, 1)
+
+
+def factor_blocks(blocks, outs, meanwhile):
     groups = BLOCK // 8
     lane = lax.broadcasted_iota(jnp.int32, (8, LANES), 1)
     sub = lax.broadcasted_iota(jnp.int32, (8, LANES), 0)
@@ -201,6 +218,8 @@
                     if r == g:
                         column = jnp.where(sub > k, column, 0.0)
                     rows[r] = rows[r] - column * scaled
+        if meanwhile:
+            meanwhile.pop(0)()
 
 
 def factor_all(mats, outs, upper):
@@ -209,6 +228,14 @@
     lane = lax.broadcasted_iota(jnp.int32, (BLOCK, LANES), 1)
     line = lax.broadcasted_iota(jnp.int32, (BLOCK, LANES), 0)
     steps = SKETCH // BLOCK
+    meanwhile = []
+
+    def update(mat, change, step, first, last):
+        rows = slice(first * BLOCK, last * BLOCK)
+        keep = lax.broadcasted_iota(jnp.int32, ((last - first) * BLOCK, PAD), 1)
+        keep = (keep < step * BLOCK) | (keep >= (step + 1) * BLOCK)
+        mat[rows, :] = jnp.where(keep, mat[rows, :], 0.0) - change
+
     for step in range(steps):
         here = slice(step * BLOCK, (step + 1) * BLOCK)
         window = slice(step // 2 * LANES, (step // 2 + 1) * LANES)
@@ -217,30 +244,37 @@
         for mat in mats:
             block = mat[here, window]
             blocks.append(pltpu.roll(block, BLOCK, 1) if odd else block)
-        factor_blocks(blocks, outs)
+        factor_blocks(blocks, outs, meanwhile)
         inside = (column >= step * BLOCK) & (column < (step + 1) * BLOCK)
         for n, (mat, out) in enumerate(zip(mats, outs)):
             both = out[...]
-            inverse = pltpu.roll(both, BLOCK, 1)[:, :BLOCK]
+            inverse = beside(pltpu.roll(both, BLOCK, 1))
             line_up = jnp.where(inside, jnp.where(column - step * BLOCK == row, 1.0, 0.0), mat[here, :])
-            panel = dot(inverse, line_up, HIGHEST)
+            panel = dot(inverse, stacked(line_up, UNDER))
             mat[here, :] = panel
             if n == 0:
                 upper[here, :] = jnp.where(column >= (step + 1) * BLOCK, panel, 0.0)
                 corner = jnp.where((lane < BLOCK) & (lane >= line), both, 0.0)
                 corner = pltpu.roll(corner, BLOCK, 1) if odd else corner
                 upper[here, window] = upper[here, window] + corner
-            if step < steps - 1:
-                start = (step + 1) * BLOCK // LANES * LANES
-                change = dot(jnp.transpose(panel[:, start:]), panel, HIGHEST)
-                below = slice((step + 1) * BLOCK, SKETCH)
-                skip = (step + 1) * BLOCK - start
-                keep = lax.broadcasted_iota(jnp.int32, (SKETCH - (step + 1) * BLOCK, PAD), 1)
-                keep = (keep < step * BLOCK) | (keep >= (step + 1) * BLOCK)
-                mat[below, :] = (
-                    jnp.where(keep, mat[below, :], 0.0)
-                    - change[skip : skip + SKETCH - (step + 1) * BLOCK]
-                )
+            if step == steps - 1:
+                continue
+            start = (step + 1) * BLOCK // LANES * LANES
+            turned = jnp.transpose(panel[:, start:])
+            turned = jnp.concatenate([turned, jnp.zeros_like(turned)], axis=1)
+            left, right = beside(turned), stacked(panel, UNDER)
+            skip = (step + 1) * BLOCK - start
+            update(mat, dot(left[skip : skip + BLOCK], right), step, step + 1, step + 2)
+            if step < steps - 2:
+
+                def rest(mat=mat, left=left, right=right, step=step, skip=skip):
+                    stop = SKETCH - start_of(step)
+                    update(mat, dot(left[skip + BLOCK : stop], right), step, step + 2, steps)
+
+                def start_of(step):
+                    return (step + 1) * BLOCK // LANES * LANES
+
+                meanwhile.append(rest)
 
 
 def columns_of(place, half, part, stream):
@@ -249,51 +283,35 @@
     return pl.ds(pl.multiple_of(first * LANES, WIDTH), WIDTH)
 
 
-def lay_out(place, members, pieces, cross):
-    for n, ((half, part, stream), piece) in enumerate(zip(members, pieces)):
-        if len(piece.shape) == 2:
-            cross[:, n * WIDTH : (n + 1) * WIDTH] = piece[...]
-            continue
-        _, mask = order(place, half, stream)
-        for slot in range(4):
-            start = n * WIDTH + (slot ^ (mask & 2)) * LANES
-            cross[:, pl.ds(pl.multiple_of(start, LANES), LANES)] = piece[slot]
-
-
-def products(place, members, cross, sketch_matrix_t, gram, coupling, left, right, mix):
+def pieces_kernel(member, id_ref, sketch_matrix_t, piece, *refs):
+    before, (terms, sums, left, right, cross, mix) = refs[:-6], refs[-6:]
+    place = coordinates(id_ref[0])
+    _, mask = order(place, member[0], member[2])
+    for slot in range(4):
+        start = (slot ^ (mask & 2)) * LANES
+        cross[:, pl.ds(pl.multiple_of(start, LANES), LANES)] = piece[slot]
     a, b, c = split(cross[...], 3)
-    for n, term in enumerate((a, b, c)):
+    for n, (term, again) in enumerate(((a, a), (b, b), (c, a))):
         left[n * SKETCH : (n + 1) * SKETCH, :] = term
+        terms[n * SKETCH : (n + 1) * SKETCH, :] = again
     right[:SKETCH, :] = a
-    right[SKETCH:PAD, :] = jnp.zeros((PAD - SKETCH, a.shape[1]), BF16)
-    for n, member in enumerate(members):
-        right[PAD:, n * WIDTH : (n + 1) * WIDTH] = sketch_matrix_t[:, columns_of(place, *member)]
+    right[SKETCH:PAD, :] = jnp.zeros((PAD - SKETCH, WIDTH), BF16)
+    right[PAD:, :] = sketch_matrix_t[:, columns_of(place, *member)]
     both = dot_nt(left[...], right[...])
-    terms = [both[n * SKETCH : (n + 1) * SKETCH] for n in range(3)]
-    for ref in (gram, coupling, mix):
+    parts = [both[n * SKETCH : (n + 1) * SKETCH] for n in range(3)]
+    mix[...] = jnp.zeros_like(mix)
+    mix[:SKETCH, :SKETCH] = parts[1][:, :SKETCH] + parts[2][:, :SKETCH]
+    mixed = (mix[...] + jnp.transpose(mix[...]))[:SKETCH]
+    sums[...] = before[0][...] if before else jnp.zeros_like(sums)
+    sums[0, :, :SKETCH] += parts[0][:, PAD:] + (parts[1][:, PAD:] + parts[2][:, PAD:])
+    sums[1, :, :SKETCH] += parts[0][:, :SKETCH] + dot_nt(b, b)
+    sums[1] += mixed
+
+
+def factor_kernel(scale, id_ref, own, other, basis_map, inverse_c, gram, coupling, upper, out0, out1, wide):
+    for n, ref in enumerate((gram, coupling)):
         ref[...] = jnp.zeros_like(ref)
-    gram[:SKETCH, :SKETCH] = terms[0][:, PAD:] + (terms[1][:, PAD:] + terms[2][:, PAD:])
-    mix[:SKETCH, :SKETCH] = terms[1][:, :SKETCH] + terms[2][:, :SKETCH]
-    coupling[:SKETCH, :SKETCH] = terms[0][:, :SKETCH] + dot_nt(b, b)
-    coupling[...] += mix[...] + jnp.transpose(mix[...])
-
-
-def pieces_kernel(members, id_ref, sketch_matrix_t, *refs):
-    pieces, (cross, *rest) = refs[: len(members)], refs[len(members) :]
-    place = coordinates(id_ref[0])
-    lay_out(place, members, pieces, cross)
-    products(place, members, cross, sketch_matrix_t, *rest)
-
-
-def factor_kernel(members, scale, id_ref, sketch_matrix_t, *refs):
-    pieces, refs = refs[: len(members)], refs[len(members) :]
-    sums, (cross, basis_map, inverse_c) = refs[:6], refs[6:9]
-    gram, coupling, left, right, mix, upper, out0, out1, wide = refs[9:]
-    place = coordinates(id_ref[0])
-    lay_out(place, members, pieces, cross)
-    products(place, members, cross, sketch_matrix_t, gram, coupling, left, right, mix)
-    gram[...] += sums[0][...] + (sums[2][...] + sums[4][...])
-    coupling[...] += sums[1][...] + (sums[3][...] + sums[5][...])
+        ref[:SKETCH, :] = own[n] + other[n]
     upper[...] = jnp.zeros_like(upper)
     factor_all((gram, coupling), (out0, out1), upper)
     row = lax.broadcasted_iota(jnp.int32, (PAD, PAD), 0)
@@ -303,22 +321,18 @@
     for n, term in enumerate((high, high, low)):
         wide[:, n * SKETCH : (n + 1) * SKETCH] = term.astype(F32)
     basis_map[...] = wide[...].astype(BF16)
-    chain = dot_nt(jnp.where(lower, coupling[...], 0.0), upper[...], HIGHEST)
-    mix[...] = dot(jnp.transpose(chain), chain, HIGHEST) * scale
-    inverse_c[...] = mix[:SKETCH, :SKETCH]
-
-
-def final_kernel(sets, id_ref, features, basis_map, inverse_c, *refs):
-    crosses, (result, stack) = refs[:-2], refs[-2:]
+    chain = dot_three(jnp.where(lower, coupling[...], 0.0), jnp.transpose(upper[...]))
+    gram[...] = dot_three(jnp.transpose(chain), chain) * scale
+    inverse_c[...] = gram[:SKETCH, :SKETCH]
+
+
+def final_kernel(members, id_ref, features, basis_map, inverse_c, *refs):
+    terms, result = refs[:-1], refs[-1]
     place = coordinates(id_ref[0])
     total = jnp.zeros(result.shape, F32)
-    for cross, members in zip(crosses, sets):
-        for n, member in enumerate(members):
-            a, b = split(cross[:, n * WIDTH : (n + 1) * WIDTH], 2)
-            for m, term in enumerate((a, b, a)):
-                stack[m * SKETCH : (m + 1) * SKETCH, :] = term
-            coeffs = dot(basis_map[...], stack[...])
-            total += dot_nt(coeffs.astype(BF16), features[:, columns_of(place, *member)])
+    for term, member in zip(terms, members):
+        coeffs = dot(basis_map[...], term[...])
+        total += dot_nt(coeffs.astype(BF16), features[:, columns_of(place, *member)])
     result[...] = dot_three(inverse_c[...], total)
 
 
@@ -355,59 +369,44 @@
     block = scatter_sum(block.reshape(8, SKETCH // 8, LANES), ("z", "z"))
     block = gather(block, ("z", "z"), 8).reshape(SKETCH, LANES)
     block = gather(block, SECOND_AXIS, 4)
-    first, second = [], []
+    streams = []
     for stream in range(2):
         own = block[2 * stream : 2 * stream + 2]
         own = jnp.concatenate([own, exchange(own, stream, 1)])
-        first.append(own)
-        second.append(exchange(own, stream, 0))
-
-    sets = [
-        ((0, 0, 0),),
-        ((0, 0, 1), (0, 1, 0), (0, 1, 1)),
-        ((1, 0, 0), (1, 0, 1)),
-        ((1, 1, 0), (1, 1, 1)),
-    ]
-    square = ((PAD, PAD), F32)
-
-    def scratch_for(members):
-        width = len(members) * WIDTH
-        return [
-            pltpu.VMEM((3 * SKETCH, width), BF16),
-            pltpu.VMEM((PAD + SKETCH, width), BF16),
-            pltpu.VMEM(*square),
-        ]
-
-    def cross_shape(members):
-        return ((SKETCH, len(members) * WIDTH), F32)
-
-    def sums_of(members, pieces):
-        return call(
-            functools.partial(pieces_kernel, members),
-            (device, sketch_matrix_t, *pieces),
-            [cross_shape(members), square, square],
-            scratch=scratch_for(members),
+        streams.append((own, exchange(own, stream, 0)))
+
+    members = [(0, part, stream) for part in range(2) for stream in range(2)]
+    terms_shape = ((3 * SKETCH, WIDTH), BF16)
+    sums_shape = ((2, SKETCH, PAD), F32)
+    terms, sums = [], ()
+    for member in members:
+        _, part, stream = member
+        term, *sums = call(
+            functools.partial(pieces_kernel, member),
+            (device, sketch_matrix_t, streams[stream][part], *sums),
+            [terms_shape, sums_shape],
+            scratch=[
+                pltpu.VMEM(*terms_shape),
+                pltpu.VMEM((PAD + SKETCH, WIDTH), BF16),
+                pltpu.VMEM((SKETCH, WIDTH), F32),
+                pltpu.VMEM((PAD, PAD), F32),
+            ],
         )
-
-    cross0, *sums0 = sums_of(sets[0], first[:1])
-    other = [across(block) for block in (cross0, first[1], *second)]
-    cross1, *sums1 = sums_of(sets[1], [first[1], *second])
-    cross2, *sums2 = sums_of(sets[2], other[:2])
-    corner = pltpu.VMEM((BLOCK, LANES), F32)
-    cross3, basis_map, inverse_c = call(
-        functools.partial(factor_kernel, sets[3], math.sqrt(rows_total)),
-        (device, sketch_matrix_t, *other[2:], *sums0, *sums1, *sums2),
-        [cross_shape(sets[3]), ((SKETCH, 3 * SKETCH), BF16), ((SKETCH, SKETCH), F32)],
-        scratch=[pltpu.VMEM(*square)] * 2
-        + scratch_for(sets[3])
-        + [pltpu.VMEM(*square), corner, corner, pltpu.VMEM((SKETCH, 3 * SKETCH), F32)],
-        flops=flops,
-    )
+        terms.append(term)
+    square, corner = pltpu.VMEM((PAD, PAD), F32), pltpu.VMEM((BLOCK, LANES), F32)
+    basis_map, inverse_c = call(
+        functools.partial(factor_kernel, math.sqrt(rows_total)),
+        (device, *sums, across(*sums)),
+        [((SKETCH, 3 * SKETCH), BF16), ((SKETCH, SKETCH), F32)],
+        scratch=[square] * 3 + [corner] * 2 + [pltpu.VMEM((SKETCH, 3 * SKETCH), F32)],
+        flops=14 * flops,
+    )
+    terms += [across(term) for term in terms]
+    members += [(1, part, stream) for _, part, stream in members]
     (result,) = call(
-        functools.partial(final_kernel, sets),
-        (device, features, basis_map, inverse_c, cross0, cross1, cross2, cross3),
+        functools.partial(final_kernel, members),
+        (device, features, basis_map, inverse_c, *terms),
         [((SKETCH, rows), F32)],
-        scratch=[pltpu.VMEM((3 * SKETCH, WIDTH), BF16)],
         flops=4 * flops,
     )
     return result.T

time: 141 us -> 134 us (0.950)
  starting transfers between devices: 27.6 us -> 19.6 us
  waiting for transfers between devices: 25.9 us -> 33.3 us
  Pallas kernels: 39.1 us -> 32.8 us
    ppermute x6 -> x7, starting transfers between devices: 22.2 us -> 14.5 us  [across(): lax.ppermute(block, 'rows', [(i, i ^ 1) for i in range(lax.axis_size('row...]
    pallas_call x7 -> x8, Pallas kernels: 39.1 us -> 32.8 us  [call(): pl.pallas_call(kernel, out_shape=[jax.ShapeDtypeStruct(shape, dtype) for...]
    ppermute x8, waiting for transfers between devices: 24.2 us -> 30.2 us  [exchange(): return lax.ppermute(block, 'rows', pairs)]
    ppermute x6 -> x7, waiting for transfers between devices: 1.68 us -> 3.1 us  [across(): lax.ppermute(block, 'rows', [(i, i ^ 1) for i in range(lax.axis_size('row...]
  transfers between devices with their start and end apart: 14 -> 15, of which waited for: 7 -> 10; matrix products, arithmetic and copies ran while one was open for 0% -> 0% of each run, Pallas kernels for 6% -> 15%
where the time goes in v2:
time: 134 us
  blocking collectives  47.5 us (35%)
  waiting for transfers between devices  33.3 us (25%)
  Pallas kernels  32.8 us (24%)
  starting transfers between devices  19.6 us (15%)
    all_to_all x4, blocking collectives, all_to_all(): lax.all_to_all(block, 'rows', 0, 0, axis_index_groups=groups, tiled=True)  47.5 us
    pallas_call x8, Pallas kernels, call(): pl.pallas_call(kernel, out_shape=[jax.ShapeDtypeStruct(shape, dtype) for...  32.8 us
    ppermute x8, waiting for transfers between devices, exchange(): return lax.ppermute(block, 'rows', pairs)  30.2 us
    ppermute x7, starting transfers between devices, across(): lax.ppermute(block, 'rows', [(i, i ^ 1) for i in range(lax.axis_size('row...  14.5 us
    ppermute x8, starting transfers between devices, exchange(): return lax.ppermute(block, 'rows', pairs)  5.1 us
    ppermute x7, waiting for transfers between devices, across(): lax.ppermute(block, 'rows', [(i, i ^ 1) for i in range(lax.axis_size('row...  3.1 us
  transfers between devices with their start and end apart: 15, of which 10 were waited for; matrix products, arithmetic and copies ran while one was open for 0% of the time, Pallas kernels for 15%

profile of v2, /device:TPU:1, one launch (start us, length us, event | category | flops | bytes accessed | tf_op | source)
XLA Modules:
  0.0 134.2 jit_solution(10370645956123049465)
XLA Ops:
  0.0 5.3 %shard_map.28 = (bf16[640,512]{1,0:T(8,128)(2,1)S(1)}, f32[8,320,128]{2,1,0:T(8,128)S(1)}, f32[8,320,128]{2,1,0:T(8,128)S(1)}) custom-call(s32[1]{0:T(128)} %bitcast.id_ref, bf16[512,4096]{1,0:T(8,128)(2,1)} %features.3, bf16[320,4096]{1,0:T(8,128)(2,1)} %bitcast.5), custom_call_target="tpu_custom_call" | custom-call | flops 2684354560 | bytes 4194304 | tf_op jit(solution)/shard_map/pallas_call | solution.py:121
  5.3 3.3 %collective-permute-start.3 = (f32[8,320,128]{2,1,0:T(8,128)S(1)}, f32[8,320,128]{2,1,0:T(8,128)S(1)}, u32[]{:S(2)}, u32[]{:S(2)}) collective-permute-start(f32[8,320,128]{2,1,0:T(8,128)S(1)} %get-tuple-element.27), channel_id=1, source_target_pairs={{0,1},{1,0},{2,3},{3,2},{4,5},{5,4},{6,7},{7,6},{8,9},{9,8},{10,11... | collective-permute-start | bytes 3932168 | tf_op jit(solution)/shard_map/ppermute | solution.py:37
  8.8 1.5 %shard_map.29 = (f32[4,320,128]{2,1,0:T(8,128)S(1)}, f32[4,320,128]{2,1,0:T(8,128)S(1)}, f32[4,320,128]{2,1,0:T(8,128)S(1)}, f32[4,320,128]{2,1,0:T(8,128)S(1)}) custom-call(s32[1]{0:T(128)} %bitcast.id_ref, bf16[512,4096]{1,0:T(8,128)(2,1)S(1)} %copy-done.1, bf16[640,512]{1,0:T(8,128)(2,1)S(1)} %get-tuple-element.22.sketches), custom_call_target="tpu_custom_call" | custom-call | flops 1342177280 | bytes 4194304 | tf_op jit(solution)/shard_map/pallas_call | solution.py:121
  10.3 1.0 collective-permute-done.3
  13.4 9.1 %collective-permute-done.4 = f32[4,320,128]{2,1,0:T(8,128)S(1)} collective-permute-done((f32[4,320,128]{2,1,0:T(8,128)S(1)}, f32[4,320,128]{2,1,0:T(8,128)S(1)}, u32[]{:S(2)}, u32[]{:S(2)}) %collective-permute-start.4) | collective-permute-done | bytes 655392 | tf_op jit(solution)/shard_map/ppermute | solution.py:48
  23.2 1.1 collective-permute-start.2
  24.3 4.5 %collective-permute-done.5 = f32[2,320,128]{2,1,0:T(8,128)S(1)} collective-permute-done((f32[2,320,128]{2,1,0:T(8,128)S(1)}, f32[2,320,128]{2,1,0:T(8,128)S(1)}, u32[]{:S(2)}, u32[]{:S(2)}) %collective-permute-start.5) | collective-permute-done | bytes 327712 | tf_op jit(solution)/shard_map/ppermute | solution.py:48
  28.9 1.8 %collective-permute-done.2 = f32[2,320,128]{2,1,0:T(8,128)S(1)} collective-permute-done((f32[2,320,128]{2,1,0:T(8,128)S(1)}, f32[2,320,128]{2,1,0:T(8,128)S(1)}, u32[]{:S(2)}, u32[]{:S(2)}) %collective-permute-start.2) | collective-permute-done | bytes 327712 | tf_op jit(solution)/shard_map/ppermute | solution.py:48
  30.8 10.5 %all_to_all.20 = f32[4,320,128]{2,1,0:T(8,128)S(1)} all-to-all(f32[4,320,128]{2,1,0:T(8,128)S(1)} %pad_maximum_fusion), channel_id=1, replica_groups={{0,2,4,6},{1,65,129,193},{3,67,131,195},{5,69,133,197},{7,71,135,199},{..., dimensions={0} | all-to-all | bytes 1310720 | tf_op jit(solution)/shard_map/all_to_all | solution.py:59
  41.4 16.3 %all_to_all.21 = f32[8,40,128]{2,1,0:T(8,128)S(1)} all-to-all(f32[8,40,128]{2,1,0:T(8,128)S(1)} %bitcast.10), channel_id=1, replica_groups={{0,8,16,24,32,40,48,56},{1,9,17,25,33,41,49,57},{2,10,18,26,34,42,50,58..., dimensions={0} | all-to-all | bytes 327680 | tf_op jit(solution)/shard_map/all_to_all | solution.py:59
  57.7 10.7 %all_to_all.22 = f32[8,40,128]{2,1,0:T(8,128)S(1)} all-to-all(f32[8,40,128]{2,1,0:T(8,128)S(1)} %broadcast_in_dim.17), channel_id=1, replica_groups={{0,8,16,24,32,40,48,56},{1,9,17,25,33,41,49,57},{2,10,18,26,34,42,50,58..., dimensions={0} | all-to-all | bytes 327680 | tf_op jit(solution)/shard_map/all_to_all | solution.py:59
  68.4 10.0 %all_to_all.23 = f32[4,320,128]{2,1,0:T(8,128)S(1)} all-to-all(f32[4,320,128]{2,1,0:T(8,128)S(1)} %broadcast_in_dim.19), channel_id=1, replica_groups={{0,2,4,6},{1,65,129,193},{3,67,131,195},{5,69,133,197},{7,71,135,199},{..., dimensions={0} | all-to-all | bytes 1310720 | tf_op jit(solution)/shard_map/all_to_all | solution.py:59
  78.5 1.9 %collective-permute-start.8 = (f32[2,320,128]{2,1,0:T(8,128)S(1)}, f32[2,320,128]{2,1,0:T(8,128)S(1)}, u32[]{:S(2)}, u32[]{:S(2)}) collective-permute-start(f32[2,320,128]{2,1,0:T(8,128)S(1)} %get-tuple-element.43), channel_id=1, source_target_pairs={{0,192},{1,7},{2,194},{3,5},{4,196},{5,3},{6,198},{7,1},{8,200},{9... | collective-permute-start | bytes 983048 | tf_op jit(solution)/shard_map/ppermute | solution.py:48
  80.5 8.3 %collective-permute-done.8 = f32[2,320,128]{2,1,0:T(8,128)S(1)} collective-permute-done((f32[2,320,128]{2,1,0:T(8,128)S(1)}, f32[2,320,128]{2,1,0:T(8,128)S(1)}, u32[]{:S(2)}, u32[]{:S(2)}) %collective-permute-start.8) | collective-permute-done | bytes 327712 | tf_op jit(solution)/shard_map/ppermute | solution.py:48
  89.0 0.9 collective-permute-start.7
  90.0 1.3 shard_map.30
  91.3 1.3 shard_map.31
  92.6 5.7 %collective-permute-done.9.piece = f32[4,320,128]{2,1,0:T(8,128)S(1)} collective-permute-done((f32[4,320,128]{2,1,0:T(8,128)S(1)}, f32[4,320,128]{2,1,0:T(8,128)S(1)}, u32[]{:S(2)}, u32[]{:S(2)}) %collective-permute-start.9) | collective-permute-done | bytes 655392 | tf_op jit(solution)/shard_map/ppermute | solution.py:48
  98.4 1.3 shard_map.32
  99.9 1.3 shard_map.33
  101.3 10.1 %collective-permute-start.10 = (f32[2,320,384]{2,1,0:T(8,128)S(1)}, f32[2,320,384]{2,1,0:T(8,128)S(1)}, u32[]{:S(2)}, u32[]{:S(2)}) collective-permute-start(f32[2,320,384]{2,1,0:T(8,128)S(1)} %get-tuple-element.32.own), channel_id=1, source_target_pairs={{0,1},{1,0},{2,3},{3,2},{4,5},{5,4},{6,7},{7,6},{8,9},{9,8},{10,11... | collective-permute-start | bytes 2949128 | tf_op jit(solution)/shard_map/ppermute | solution.py:37
  112.4 1.2 collective-permute-done.10.other
  113.5 14.4 %shard_map.34 = (bf16[320,960]{1,0:T(8,128)(2,1)S(1)}, f32[320,320]{1,0:T(8,128)S(1)}) custom-call(s32[1]{0:T(128)} %bitcast.id_ref, f32[2,320,384]{2,1,0:T(8,128)S(1)} %get-tuple-element.32.own, f32[2,320,384]{2,1,0:T(8,128)S(1)} %collective-permute-done.10.other), custom_call_target="tpu_custom_call" | custom-call | flops 18790481920 | bytes 4194304 | tf_op jit(solution)/shard_map/pallas_call | solution.py:121
  128.0 6.2 %shard_map.35 = f32[320,512]{1,0:T(8,128)} custom-call(s32[1]{0:T(128)} %bitcast.id_ref, bf16[512,4096]{1,0:T(8,128)(2,1)S(1)} %copy-done.2, bf16[320,960]{1,0:T(8,128)(2,1)S(1)} %get-tuple-element.33.basis_map, f32[320,320]{1,0:T(8,128)S(1)} %get-tuple-element.34.inverse_c, bf16[960,512]{1,0:T(8,128)(2,1)S(1)} %get-tuple-element.35.refs_0_, ...), custom_call_target="tpu_custom_call" | custom-call | flops 5368709120 | bytes 4194304 | tf_op jit(solution)/shard_map/pallas_call | solution.py:121
  (38 shorter events, 4.7 us)
Async XLA Ops:
  0.0 8.8 %copy-start.1 = (bf16[512,4096]{1,0:T(8,128)(2,1)S(1)}, bf16[512,4096]{1,0:T(8,128)(2,1)}, u32[]{:S(2)}) copy-start(bf16[512,4096]{1,0:T(8,128)(2,1)} %features.3) | copy-start | bytes 12582916
  5.3 6.0 %collective-permute-start.3 = (f32[8,320,128]{2,1,0:T(8,128)S(1)}, f32[8,320,128]{2,1,0:T(8,128)S(1)}, u32[]{:S(2)}, u32[]{:S(2)}) collective-permute-start(f32[8,320,128]{2,1,0:T(8,128)S(1)} %get-tuple-element.27), channel_id=1, source_target_pairs={{0,1},{1,0},{2,3},{3,2},{4,5},{5,4},{6,7},{7,6},{8,9},{9,8},{10,11... | collective-permute-start | bytes 3932168 | tf_op jit(solution)/shard_map/ppermute | solution.py:37
  8.7 4.5 %collective-permute-start = (f32[8,320,128]{2,1,0:T(8,128)S(1)}, f32[8,320,128]{2,1,0:T(8,128)S(1)}, u32[]{:S(2)}, u32[]{:S(2)}) collective-permute-start(f32[8,320,128]{2,1,0:T(8,128)S(1)} %get-tuple-element.24), channel_id=1, source_target_pairs={{0,1},{1,0},{2,3},{3,2},{4,5},{5,4},{6,7},{7,6},{8,9},{9,8},{10,11... | collective-permute-start | bytes 3932168 | tf_op jit(solution)/shard_map/ppermute | solution.py:37
  11.4 11.0 %collective-permute-start.4 = (f32[4,320,128]{2,1,0:T(8,128)S(1)}, f32[4,320,128]{2,1,0:T(8,128)S(1)}, u32[]{:S(2)}, u32[]{:S(2)}) collective-permute-start(f32[4,320,128]{2,1,0:T(8,128)S(1)} %get-tuple-element.42), channel_id=1, source_target_pairs={{0,192},{1,7},{2,194},{3,5},{4,196},{5,3},{6,198},{7,1},{8,200},{9... | collective-permute-start | bytes 1966088 | tf_op jit(solution)/shard_map/ppermute | solution.py:48
  13.3 9.8 %collective-permute-start.1 = (f32[4,320,128]{2,1,0:T(8,128)S(1)}, f32[4,320,128]{2,1,0:T(8,128)S(1)}, u32[]{:S(2)}, u32[]{:S(2)}) collective-permute-start(f32[4,320,128]{2,1,0:T(8,128)S(1)} %get-tuple-element.40), channel_id=1, source_target_pairs={{0,64},{1,3},{2,66},{3,1},{4,68},{5,7},{6,70},{7,5},{8,72},{9,11},... | collective-permute-start | bytes 1966088 | tf_op jit(solution)/shard_map/ppermute | solution.py:48
  22.5 6.3 %collective-permute-start.5 = (f32[2,320,128]{2,1,0:T(8,128)S(1)}, f32[2,320,128]{2,1,0:T(8,128)S(1)}, u32[]{:S(2)}, u32[]{:S(2)}) collective-permute-start(f32[2,320,128]{2,1,0:T(8,128)S(1)} %slice_add_fusion.4), channel_id=1, source_target_pairs={{0,64},{1,3},{2,66},{3,1},{4,68},{5,7},{6,70},{7,5},{8,72},{9,11},... | collective-permute-start | bytes 983048 | tf_op jit(solution)/shard_map/ppermute | solution.py:48
  23.2 7.5 %collective-permute-start.2 = (f32[2,320,128]{2,1,0:T(8,128)S(1)}, f32[2,320,128]{2,1,0:T(8,128)S(1)}, u32[]{:S(2)}, u32[]{:S(2)}) collective-permute-start(f32[2,320,128]{2,1,0:T(8,128)S(1)} %slice_add_fusion.6), channel_id=1, source_target_pairs={{0,192},{1,7},{2,194},{3,5},{4,196},{5,3},{6,198},{7,1},{8,200},{9... | collective-permute-start | bytes 983048 | tf_op jit(solution)/shard_map/ppermute | solution.py:48
  78.5 10.3 %collective-permute-start.8 = (f32[2,320,128]{2,1,0:T(8,128)S(1)}, f32[2,320,128]{2,1,0:T(8,128)S(1)}, u32[]{:S(2)}, u32[]{:S(2)}) collective-permute-start(f32[2,320,128]{2,1,0:T(8,128)S(1)} %get-tuple-element.43), channel_id=1, source_target_pairs={{0,192},{1,7},{2,194},{3,5},{4,196},{5,3},{6,198},{7,1},{8,200},{9... | collective-permute-start | bytes 983048 | tf_op jit(solution)/shard_map/ppermute | solution.py:48
  80.5 9.5 %copy-start = (bf16[4096,320]{0,1:T(8,128)(2,1)S(1)}, bf16[4096,320]{0,1:T(8,128)(2,1)}, u32[]{:S(2)}) copy-start(bf16[4096,320]{0,1:T(8,128)(2,1)} %param.3) | copy-start | bytes 7864324
  80.5 8.5 %collective-permute-start.6 = (f32[2,320,128]{2,1,0:T(8,128)S(1)}, f32[2,320,128]{2,1,0:T(8,128)S(1)}, u32[]{:S(2)}, u32[]{:S(2)}) collective-permute-start(f32[2,320,128]{2,1,0:T(8,128)S(1)} %get-tuple-element.44), channel_id=1, source_target_pairs={{0,64},{1,3},{2,66},{3,1},{4,68},{5,7},{6,70},{7,5},{8,72},{9,11},... | collective-permute-start | bytes 983048 | tf_op jit(solution)/shard_map/ppermute | solution.py:48
  88.9 9.5 %collective-permute-start.9 = (f32[4,320,128]{2,1,0:T(8,128)S(1)}, f32[4,320,128]{2,1,0:T(8,128)S(1)}, u32[]{:S(2)}, u32[]{:S(2)}) collective-permute-start(f32[4,320,128]{2,1,0:T(8,128)S(1)} %pad_maximum_fusion.2.piece), channel_id=1, source_target_pairs={{0,64},{1,3},{2,66},{3,1},{4,68},{5,7},{6,70},{7,5},{8,72},{9,11},... | collective-permute-start | bytes 1966088 | tf_op jit(solution)/shard_map/ppermute | solution.py:48
  89.0 10.9 %collective-permute-start.7 = (f32[4,320,128]{2,1,0:T(8,128)S(1)}, f32[4,320,128]{2,1,0:T(8,128)S(1)}, u32[]{:S(2)}, u32[]{:S(2)}) collective-permute-start(f32[4,320,128]{2,1,0:T(8,128)S(1)} %pad_maximum_fusion.1.piece), channel_id=1, source_target_pairs={{0,192},{1,7},{2,194},{3,5},{4,196},{5,3},{6,198},{7,1},{8,200},{9... | collective-permute-start | bytes 1966088 | tf_op jit(solution)/shard_map/ppermute | solution.py:48
  101.3 12.3 %collective-permute-start.10 = (f32[2,320,384]{2,1,0:T(8,128)S(1)}, f32[2,320,384]{2,1,0:T(8,128)S(1)}, u32[]{:S(2)}, u32[]{:S(2)}) collective-permute-start(f32[2,320,384]{2,1,0:T(8,128)S(1)} %get-tuple-element.32.own), channel_id=1, source_target_pairs={{0,1},{1,0},{2,3},{3,2},{4,5},{5,4},{6,7},{7,6},{8,9},{9,8},{10,11... | collective-permute-start | bytes 2949128 | tf_op jit(solution)/shard_map/ppermute | solution.py:37
  111.4 16.6 %collective-permute-start.12 = (bf16[960,512]{1,0:T(8,128)(2,1)S(1)}, bf16[960,512]{1,0:T(8,128)(2,1)S(1)}, u32[]{:S(2)}, u32[]{:S(2)}) collective-permute-start(bf16[960,512]{1,0:T(8,128)(2,1)S(1)} %get-tuple-element.36.refs_1_), channel_id=1, source_target_pairs={{0,1},{1,0},{2,3},{3,2},{4,5},{5,4},{6,7},{7,6},{8,9},{9,8},{10,11... | collective-permute-start | bytes 2949128 | tf_op jit(solution)/shard_map/ppermute | solution.py:37
  111.5 16.5 %collective-permute-start.11 = (bf16[960,512]{1,0:T(8,128)(2,1)S(1)}, bf16[960,512]{1,0:T(8,128)(2,1)S(1)}, u32[]{:S(2)}, u32[]{:S(2)}) collective-permute-start(bf16[960,512]{1,0:T(8,128)(2,1)S(1)} %get-tuple-element.35.refs_0_), channel_id=1, source_target_pairs={{0,1},{1,0},{2,3},{3,2},{4,5},{5,4},{6,7},{7,6},{8,9},{9,8},{10,11... | collective-permute-start | bytes 2949128 | tf_op jit(solution)/shard_map/ppermute | solution.py:37
  111.9 16.1 %collective-permute-start.14 = (bf16[960,512]{1,0:T(8,128)(2,1)S(1)}, bf16[960,512]{1,0:T(8,128)(2,1)S(1)}, u32[]{:S(2)}, u32[]{:S(2)}) collective-permute-start(bf16[960,512]{1,0:T(8,128)(2,1)S(1)} %get-tuple-element.38.refs_3_), channel_id=1, source_target_pairs={{0,1},{1,0},{2,3},{3,2},{4,5},{5,4},{6,7},{7,6},{8,9},{9,8},{10,11... | collective-permute-start | bytes 2949128 | tf_op jit(solution)/shard_map/ppermute | solution.py:37
  112.0 16.0 %copy-start.2 = (bf16[512,4096]{1,0:T(8,128)(2,1)S(1)}, bf16[512,4096]{1,0:T(8,128)(2,1)}, u32[]{:S(2)}) copy-start(bf16[512,4096]{1,0:T(8,128)(2,1)} %features.3) | copy-start | bytes 12582916
  112.0 16.0 %collective-permute-start.13 = (bf16[960,512]{1,0:T(8,128)(2,1)S(1)}, bf16[960,512]{1,0:T(8,128)(2,1)S(1)}, u32[]{:S(2)}, u32[]{:S(2)}) collective-permute-start(bf16[960,512]{1,0:T(8,128)(2,1)S(1)} %get-tuple-element.37.refs_2_), channel_id=1, source_target_pairs={{0,1},{1,0},{2,3},{3,2},{4,5},{5,4},{6,7},{7,6},{8,9},{9,8},{10,11... | collective-permute-start | bytes 2949128 | tf_op jit(solution)/shard_map/ppermute | solution.py:37

commit v3 on v2

--- a/solution.py
+++ b/solution.py
@@ -48,23 +48,14 @@
     return lax.ppermute(block, "rows", pairs)
 
 
-def all_to_all(block, axes):
-    size = block.shape[0]
+def all_to_all(block):
     groups = []
     for i in range(lax.axis_size("rows")):
         place = coordinates(i)
-        axis = axes[place["c"]]
-        if place[axis] == 0:
-            groups.append([device_at({**place, axis: k}) for k in range(size)])
+        axis = SECOND_AXIS[place["c"]]
+        if place[axis] == 0 and place["z"] == 0:
+            groups.append([device_at({**place, axis: a, "z": z}) for a in range(4) for z in range(8)])
     return lax.all_to_all(block, "rows", 0, 0, axis_index_groups=groups, tiled=True)
-
-
-def scatter_sum(block, axes):
-    return jnp.sum(all_to_all(block, axes), axis=0)
-
-
-def gather(block, axes, size):
-    return all_to_all(jnp.broadcast_to(block[None], (size, *block.shape)), axes)
 
 
 def order(place, half, stream):
@@ -88,26 +79,21 @@
 
 
 def send_kernel(id_ref, features_hbm, matrix_hbm, sketches, send0, send1, features, matrix, sems):
-    chunks = sems.shape[1]
-    width = features.shape[1] // chunks
-    copies = []
+    chunks = sems.shape[0] - 1
+    height = features.shape[0] // chunks
+    copies = [pltpu.make_async_copy(matrix_hbm, matrix, sems.at[chunks])]
     for n in range(chunks):
-        columns = slice(n * width, (n + 1) * width)
-        pair = [
-            pltpu.make_async_copy(source.at[:, columns], target.at[:, columns], sems.at[m, n])
-            for m, (source, target) in enumerate(((matrix_hbm, matrix), (features_hbm, features)))
-        ]
-        for copy in pair:
-            copy.start()
-        copies.append((columns, pair))
-    sketch_t = jnp.zeros((SKETCH, features.shape[0]), F32)
-    for columns, pair in copies:
-        for copy in pair:
-            copy.wait()
-        sketch_t += dot_nt(matrix[:, columns], features[:, columns])
-    high, low = split(sketch_t, 2)
-    sketches[:SKETCH, :] = high
-    sketches[SKETCH:, :] = low
+        rows = slice(n * height, (n + 1) * height)
+        copies.append(pltpu.make_async_copy(features_hbm.at[rows], features.at[rows], sems.at[n]))
+    for copy in copies:
+        copy.start()
+    copies[0].wait()
+    for n in range(chunks):
+        copies[n + 1].wait()
+        rows = slice(n * height, (n + 1) * height)
+        high, low = split(dot_nt(matrix[...], features[rows, :]), 2)
+        sketches[:SKETCH, rows] = high
+        sketches[SKETCH:, rows] = low
     cross_blocks(id_ref, features, sketches, (((1, 0, 0), send0), ((1, 1, 0), send1)))
 
 
@@ -327,13 +313,12 @@
 
 
 def final_kernel(members, id_ref, features, basis_map, inverse_c, *refs):
-    terms, result = refs[:-1], refs[-1]
+    terms, (result, coeffs) = refs[:-2], refs[-2:]
     place = coordinates(id_ref[0])
-    total = jnp.zeros(result.shape, F32)
     for term, member in zip(terms, members):
-        coeffs = dot(basis_map[...], term[...])
-        total += dot_nt(coeffs.astype(BF16), features[:, columns_of(place, *member)])
-    result[...] = dot_three(inverse_c[...], total)
+        coeffs[:, columns_of(place, *member)] = dot(basis_map[...], term[...]).astype(BF16)
+    projected = dot_nt(coeffs[...], features[...])
+    result[...] = dot_three(inverse_c[...], projected)
 
 
 def body(features, sketch_matrix):
@@ -352,7 +337,7 @@
         scratch=[
             pltpu.VMEM((rows, width), BF16),
             pltpu.VMEM((SKETCH, width), BF16),
-            pltpu.SemaphoreType.DMA((2, 4)),
+            pltpu.SemaphoreType.DMA((3,)),
         ],
         flops=2 * flops,
         space=pltpu.HBM,
@@ -365,10 +350,9 @@
     block = jnp.concatenate(
         [scatter_stream(0, low0, high0, received[0]), scatter_stream(1, low1, high1, received[1])]
     )
-    block = scatter_sum(block, SECOND_AXIS)
-    block = scatter_sum(block.reshape(8, SKETCH // 8, LANES), ("z", "z"))
-    block = gather(block, ("z", "z"), 8).reshape(SKETCH, LANES)
-    block = gather(block, SECOND_AXIS, 4)
+    block = jnp.sum(all_to_all(block.reshape(32, SKETCH // 8, LANES)), axis=0)
+    block = all_to_all(jnp.broadcast_to(block[None], (32, *block.shape)))
+    block = block.reshape(4, SKETCH, LANES)
     streams = []
     for stream in range(2):
         own = block[2 * stream : 2 * stream + 2]
@@ -407,6 +391,7 @@
         functools.partial(final_kernel, members),
         (device, features, basis_map, inverse_c, *terms),
         [((SKETCH, rows), F32)],
+        scratch=[pltpu.VMEM((SKETCH, width), BF16)],
         flops=4 * flops,
     )
     return result.T

time: 134 us -> 133 us (level)
  starting transfers between devices: 19.6 us -> 14.3 us
  blocking collectives: 47.5 us -> 50.6 us
  Pallas kernels: 32.8 us -> 34.7 us
  waiting for transfers between devices: 33.3 us -> 31.9 us
    ppermute x7, starting transfers between devices: 14.5 us -> 10.3 us  [across(): lax.ppermute(block, 'rows', [(i, i ^ 1) for i in range(lax.axis_size('row...]
    all_to_all x4 -> x2, blocking collectives: 47.5 us -> 50.6 us  [all_to_all(): lax.all_to_all(block, 'rows', 0, 0, axis_index_groups=groups, tiled=True)]
    pallas_call x8, Pallas kernels: 32.8 us -> 34.7 us  [call(): pl.pallas_call(kernel, out_shape=[jax.ShapeDtypeStruct(shape, dtype) for...]
    ppermute x8, waiting for transfers between devices: 30.2 us -> 28.8 us  [exchange(): return lax.ppermute(block, 'rows', pairs)]
where the time goes in v3:
time: 133 us; the launch traced here: 132 us
  blocking collectives  50.6 us (38%)
  Pallas kernels  34.7 us (26%)
  waiting for transfers between devices  31.9 us (24%)
  starting transfers between devices  14.3 us (11%)
    all_to_all x2, blocking collectives, all_to_all(): lax.all_to_all(block, 'rows', 0, 0, axis_index_groups=groups, tiled=True)  50.6 us
    pallas_call x8, Pallas kernels, call(): pl.pallas_call(kernel, out_shape=[jax.ShapeDtypeStruct(shape, dtype) for...  34.7 us
    ppermute x8, waiting for transfers between devices, exchange(): return lax.ppermute(block, 'rows', pairs)  28.8 us
    ppermute x7, starting transfers between devices, across(): lax.ppermute(block, 'rows', [(i, i ^ 1) for i in range(lax.axis_size('row...  10.3 us
    ppermute x8, starting transfers between devices, exchange(): return lax.ppermute(block, 'rows', pairs)  3.98 us
    ppermute x7, waiting for transfers between devices, across(): lax.ppermute(block, 'rows', [(i, i ^ 1) for i in range(lax.axis_size('row...  3.11 us
  transfers between devices with their start and end apart: 15, of which 10 were waited for; matrix products, arithmetic and copies ran while one was open for 0% of the time, Pallas kernels for 15%

profile of v3, /device:TPU:1, one launch (start us, length us, event | category | flops | bytes accessed | tf_op | source)
XLA Modules:
  0.0 132.5 jit_solution(3218080516974718459)
XLA Ops:
  0.0 7.3 %shard_map.28 = (bf16[640,512]{1,0:T(8,128)(2,1)S(1)}, f32[8,320,128]{2,1,0:T(8,128)S(1)}, f32[8,320,128]{2,1,0:T(8,128)S(1)}) custom-call(s32[1]{0:T(128)} %bitcast.id_ref, bf16[512,4096]{1,0:T(8,128)(2,1)} %features.3, bf16[320,4096]{1,0:T(8,128)(2,1)} %bitcast.6), custom_call_target="tpu_custom_call" | custom-call | flops 2684354560 | bytes 4194304 | tf_op jit(solution)/shard_map/pallas_call | solution.py:107
  7.3 3.3 %collective-permute-start.3 = (f32[8,320,128]{2,1,0:T(8,128)S(1)}, f32[8,320,128]{2,1,0:T(8,128)S(1)}, u32[]{:S(2)}, u32[]{:S(2)}) collective-permute-start(f32[8,320,128]{2,1,0:T(8,128)S(1)} %get-tuple-element.27), channel_id=1, source_target_pairs={{0,1},{1,0},{2,3},{3,2},{4,5},{5,4},{6,7},{7,6},{8,9},{9,8},{10,11... | collective-permute-start | bytes 3932168 | tf_op jit(solution)/shard_map/ppermute | solution.py:37
  10.7 1.5 %shard_map.29 = (f32[4,320,128]{2,1,0:T(8,128)S(1)}, f32[4,320,128]{2,1,0:T(8,128)S(1)}, f32[4,320,128]{2,1,0:T(8,128)S(1)}, f32[4,320,128]{2,1,0:T(8,128)S(1)}) custom-call(s32[1]{0:T(128)} %bitcast.id_ref, bf16[512,4096]{1,0:T(8,128)(2,1)S(1)} %copy-done.1, bf16[640,512]{1,0:T(8,128)(2,1)S(1)} %get-tuple-element.22.sketches), custom_call_target="tpu_custom_call" | custom-call | flops 1342177280 | bytes 4194304 | tf_op jit(solution)/shard_map/pallas_call | solution.py:107
  12.3 1.0 collective-permute-done.3
  13.4 0.8 collective-permute-start.4
  14.3 0.9 collective-permute-done
  15.4 9.1 %collective-permute-done.4 = f32[4,320,128]{2,1,0:T(8,128)S(1)} collective-permute-done((f32[4,320,128]{2,1,0:T(8,128)S(1)}, f32[4,320,128]{2,1,0:T(8,128)S(1)}, u32[]{:S(2)}, u32[]{:S(2)}) %collective-permute-start.4) | collective-permute-done | bytes 655392 | tf_op jit(solution)/shard_map/ppermute | solution.py:48
  24.6 0.5 collective-permute-done.1
  25.2 1.1 collective-permute-start.2
  26.3 4.5 %collective-permute-done.5 = f32[2,320,128]{2,1,0:T(8,128)S(1)} collective-permute-done((f32[2,320,128]{2,1,0:T(8,128)S(1)}, f32[2,320,128]{2,1,0:T(8,128)S(1)}, u32[]{:S(2)}, u32[]{:S(2)}) %collective-permute-start.5) | collective-permute-done | bytes 327712 | tf_op jit(solution)/shard_map/ppermute | solution.py:48
  30.9 1.8 %collective-permute-done.2 = f32[2,320,128]{2,1,0:T(8,128)S(1)} collective-permute-done((f32[2,320,128]{2,1,0:T(8,128)S(1)}, f32[2,320,128]{2,1,0:T(8,128)S(1)}, u32[]{:S(2)}, u32[]{:S(2)}) %collective-permute-start.2) | collective-permute-done | bytes 327712 | tf_op jit(solution)/shard_map/ppermute | solution.py:48
  32.8 26.1 %all_to_all.10 = f32[32,40,128]{2,1,0:T(8,128)S(1)} all-to-all(f32[32,40,128]{2,1,0:T(8,128)S(1)} %bitcast.11), channel_id=1, replica_groups={{0,8,16,24,32,40,48,56,2,10,18,26,34,42,50,58,4,12,20,28,36,44,52,60,6,..., dimensions={0} | all-to-all | bytes 1310720 | tf_op jit(solution)/shard_map/all_to_all | solution.py:58
  59.0 24.5 %all_to_all.11 = f32[32,40,128]{2,1,0:T(8,128)S(1)} all-to-all(f32[32,40,128]{2,1,0:T(8,128)S(1)} %broadcast_in_dim.10), channel_id=1, replica_groups={{0,8,16,24,32,40,48,56,2,10,18,26,34,42,50,58,4,12,20,28,36,44,52,60,6,..., dimensions={0} | all-to-all | bytes 1310720 | tf_op jit(solution)/shard_map/all_to_all | solution.py:58
  83.8 7.3 %collective-permute-done.8 = f32[2,320,128]{2,1,0:T(8,128)S(1)} collective-permute-done((f32[2,320,128]{2,1,0:T(8,128)S(1)}, f32[2,320,128]{2,1,0:T(8,128)S(1)}, u32[]{:S(2)}, u32[]{:S(2)}) %collective-permute-start.8) | collective-permute-done | bytes 327712 | tf_op jit(solution)/shard_map/ppermute | solution.py:48
  91.3 1.6 %collective-permute-start.7 = (f32[4,320,128]{2,1,0:T(8,128)S(1)}, f32[4,320,128]{2,1,0:T(8,128)S(1)}, u32[]{:S(2)}, u32[]{:S(2)}) collective-permute-start(f32[4,320,128]{2,1,0:T(8,128)S(1)} %pad_maximum_fusion.1.piece), channel_id=1, source_target_pairs={{0,192},{1,7},{2,194},{3,5},{4,196},{5,3},{6,198},{7,1},{8,200},{9... | collective-permute-start | bytes 1966088 | tf_op jit(solution)/shard_map/ppermute | solution.py:48
  92.9 1.3 shard_map.30
  94.2 1.3 %shard_map.31 = (bf16[960,512]{1,0:T(8,128)(2,1)S(1)}, f32[2,320,384]{2,1,0:T(8,128)S(1)}) custom-call(s32[1]{0:T(128)} %bitcast.id_ref, bf16[320,4096]{1,0:T(8,128)(2,1)S(1)} %bitcast.8, f32[4,320,128]{2,1,0:T(8,128)S(1)} %pad_maximum_fusion.1.piece, f32[2,320,384]{2,1,0:T(8,128)S(1)} %get-tuple-element.29.refs_0_), custom_call_target="tpu_custom_call" | custom-call | bytes 4194304 | tf_op jit(solution)/shard_map/pallas_call | solution.py:107
  95.5 5.4 %collective-permute-done.9.piece = f32[4,320,128]{2,1,0:T(8,128)S(1)} collective-permute-done((f32[4,320,128]{2,1,0:T(8,128)S(1)}, f32[4,320,128]{2,1,0:T(8,128)S(1)}, u32[]{:S(2)}, u32[]{:S(2)}) %collective-permute-start.9) | collective-permute-done | bytes 655392 | tf_op jit(solution)/shard_map/ppermute | solution.py:48
  100.9 1.3 %shard_map.32 = (bf16[960,512]{1,0:T(8,128)(2,1)S(1)}, f32[2,320,384]{2,1,0:T(8,128)S(1)}) custom-call(s32[1]{0:T(128)} %bitcast.id_ref, bf16[320,4096]{1,0:T(8,128)(2,1)S(1)} %bitcast.9, f32[4,320,128]{2,1,0:T(8,128)S(1)} %collective-permute-done.9.piece, f32[2,320,384]{2,1,0:T(8,128)S(1)} %get-tuple-element.30.refs_0_), custom_call_target="tpu_custom_call" | custom-call | bytes 4194304 | tf_op jit(solution)/shard_map/pallas_call | solution.py:107
  102.5 1.3 %shard_map.33 = (bf16[960,512]{1,0:T(8,128)(2,1)S(1)}, f32[2,320,384]{2,1,0:T(8,128)S(1)}) custom-call(s32[1]{0:T(128)} %bitcast.id_ref, bf16[320,4096]{1,0:T(8,128)(2,1)S(1)} %bitcast.10, f32[4,320,128]{2,1,0:T(8,128)S(1)} %collective-permute-done.7.piece, f32[2,320,384]{2,1,0:T(8,128)S(1)} %get-tuple-element.31.refs_0_), custom_call_target="tpu_custom_call" | custom-call | bytes 4194304 | tf_op jit(solution)/shard_map/pallas_call | solution.py:107
  103.8 5.9 %collective-permute-start.10 = (f32[2,320,384]{2,1,0:T(8,128)S(1)}, f32[2,320,384]{2,1,0:T(8,128)S(1)}, u32[]{:S(2)}, u32[]{:S(2)}) collective-permute-start(f32[2,320,384]{2,1,0:T(8,128)S(1)} %get-tuple-element.32.own), channel_id=1, source_target_pairs={{0,1},{1,0},{2,3},{3,2},{4,5},{5,4},{6,7},{7,6},{8,9},{9,8},{10,11... | collective-permute-start | bytes 2949128 | tf_op jit(solution)/shard_map/ppermute | solution.py:37
  110.8 1.2 collective-permute-done.10.other
  111.9 14.4 %shard_map.34 = (bf16[320,960]{1,0:T(8,128)(2,1)S(1)}, f32[320,320]{1,0:T(8,128)S(1)}) custom-call(s32[1]{0:T(128)} %bitcast.id_ref, f32[2,320,384]{2,1,0:T(8,128)S(1)} %get-tuple-element.32.own, f32[2,320,384]{2,1,0:T(8,128)S(1)} %collective-permute-done.10.other), custom_call_target="tpu_custom_call" | custom-call | flops 18790481920 | bytes 4194304 | tf_op jit(solution)/shard_map/pallas_call | solution.py:107
  126.4 6.1 %shard_map.35 = f32[320,512]{1,0:T(8,128)} custom-call(s32[1]{0:T(128)} %bitcast.id_ref, bf16[512,4096]{1,0:T(8,128)(2,1)S(1)} %copy-done.2, bf16[320,960]{1,0:T(8,128)(2,1)S(1)} %get-tuple-element.33.basis_map, f32[320,320]{1,0:T(8,128)S(1)} %get-tuple-element.34.inverse_c, bf16[960,512]{1,0:T(8,128)(2,1)S(1)} %get-tuple-element.35.refs_0_, ...), custom_call_target="tpu_custom_call" | custom-call | flops 5368709120 | bytes 4194304 | tf_op jit(solution)/shard_map/pallas_call | solution.py:107
  (34 shorter events, 2.6 us)
Async XLA Ops:
  0.0 10.7 %copy-start.1 = (bf16[512,4096]{1,0:T(8,128)(2,1)S(1)}, bf16[512,4096]{1,0:T(8,128)(2,1)}, u32[]{:S(2)}) copy-start(bf16[512,4096]{1,0:T(8,128)(2,1)} %features.3) | copy-start | bytes 12582916
  7.3 6.0 %collective-permute-start.3 = (f32[8,320,128]{2,1,0:T(8,128)S(1)}, f32[8,320,128]{2,1,0:T(8,128)S(1)}, u32[]{:S(2)}, u32[]{:S(2)}) collective-permute-start(f32[8,320,128]{2,1,0:T(8,128)S(1)} %get-tuple-element.27), channel_id=1, source_target_pairs={{0,1},{1,0},{2,3},{3,2},{4,5},{5,4},{6,7},{7,6},{8,9},{9,8},{10,11... | collective-permute-start | bytes 3932168 | tf_op jit(solution)/shard_map/ppermute | solution.py:37
  10.6 4.5 %collective-permute-start = (f32[8,320,128]{2,1,0:T(8,128)S(1)}, f32[8,320,128]{2,1,0:T(8,128)S(1)}, u32[]{:S(2)}, u32[]{:S(2)}) collective-permute-start(f32[8,320,128]{2,1,0:T(8,128)S(1)} %get-tuple-element.24), channel_id=1, source_target_pairs={{0,1},{1,0},{2,3},{3,2},{4,5},{5,4},{6,7},{7,6},{8,9},{9,8},{10,11... | collective-permute-start | bytes 3932168 | tf_op jit(solution)/shard_map/ppermute | solution.py:37
  13.4 11.0 %collective-permute-start.4 = (f32[4,320,128]{2,1,0:T(8,128)S(1)}, f32[4,320,128]{2,1,0:T(8,128)S(1)}, u32[]{:S(2)}, u32[]{:S(2)}) collective-permute-start(f32[4,320,128]{2,1,0:T(8,128)S(1)} %get-tuple-element.42), channel_id=1, source_target_pairs={{0,192},{1,7},{2,194},{3,5},{4,196},{5,3},{6,198},{7,1},{8,200},{9... | collective-permute-start | bytes 1966088 | tf_op jit(solution)/shard_map/ppermute | solution.py:48
  15.3 9.8 %collective-permute-start.1 = (f32[4,320,128]{2,1,0:T(8,128)S(1)}, f32[4,320,128]{2,1,0:T(8,128)S(1)}, u32[]{:S(2)}, u32[]{:S(2)}) collective-permute-start(f32[4,320,128]{2,1,0:T(8,128)S(1)} %get-tuple-element.40), channel_id=1, source_target_pairs={{0,64},{1,3},{2,66},{3,1},{4,68},{5,7},{6,70},{7,5},{8,72},{9,11},... | collective-permute-start | bytes 1966088 | tf_op jit(solution)/shard_map/ppermute | solution.py:48
  24.5 6.3 %collective-permute-start.5 = (f32[2,320,128]{2,1,0:T(8,128)S(1)}, f32[2,320,128]{2,1,0:T(8,128)S(1)}, u32[]{:S(2)}, u32[]{:S(2)}) collective-permute-start(f32[2,320,128]{2,1,0:T(8,128)S(1)} %slice_add_fusion.4), channel_id=1, source_target_pairs={{0,64},{1,3},{2,66},{3,1},{4,68},{5,7},{6,70},{7,5},{8,72},{9,11},... | collective-permute-start | bytes 983048 | tf_op jit(solution)/shard_map/ppermute | solution.py:48
  25.2 7.5 %collective-permute-start.2 = (f32[2,320,128]{2,1,0:T(8,128)S(1)}, f32[2,320,128]{2,1,0:T(8,128)S(1)}, u32[]{:S(2)}, u32[]{:S(2)}) collective-permute-start(f32[2,320,128]{2,1,0:T(8,128)S(1)} %slice_add_fusion.6), channel_id=1, source_target_pairs={{0,192},{1,7},{2,194},{3,5},{4,196},{5,3},{6,198},{7,1},{8,200},{9... | collective-permute-start | bytes 983048 | tf_op jit(solution)/shard_map/ppermute | solution.py:48
  83.6 7.5 %collective-permute-start.8 = (f32[2,320,128]{2,1,0:T(8,128)S(1)}, f32[2,320,128]{2,1,0:T(8,128)S(1)}, u32[]{:S(2)}, u32[]{:S(2)}) collective-permute-start(f32[2,320,128]{2,1,0:T(8,128)S(1)} %bitcast.14), channel_id=1, source_target_pairs={{0,192},{1,7},{2,194},{3,5},{4,196},{5,3},{6,198},{7,1},{8,200},{9... | collective-permute-start | bytes 983048 | tf_op jit(solution)/shard_map/ppermute | solution.py:48
  83.7 9.2 %copy-start = (bf16[4096,320]{0,1:T(8,128)(2,1)S(1)}, bf16[4096,320]{0,1:T(8,128)(2,1)}, u32[]{:S(2)}) copy-start(bf16[4096,320]{0,1:T(8,128)(2,1)} %param.3) | copy-start | bytes 7864324
  83.7 7.6 %collective-permute-start.6 = (f32[2,320,128]{2,1,0:T(8,128)S(1)}, f32[2,320,128]{2,1,0:T(8,128)S(1)}, u32[]{:S(2)}, u32[]{:S(2)}) collective-permute-start(f32[2,320,128]{2,1,0:T(8,128)S(1)} %bitcast.12), channel_id=1, source_target_pairs={{0,64},{1,3},{2,66},{3,1},{4,68},{5,7},{6,70},{7,5},{8,72},{9,11},... | collective-permute-start | bytes 983048 | tf_op jit(solution)/shard_map/ppermute | solution.py:48
  91.1 9.8 %collective-permute-start.9 = (f32[4,320,128]{2,1,0:T(8,128)S(1)}, f32[4,320,128]{2,1,0:T(8,128)S(1)}, u32[]{:S(2)}, u32[]{:S(2)}) collective-permute-start(f32[4,320,128]{2,1,0:T(8,128)S(1)} %pad_maximum_fusion.2.piece), channel_id=1, source_target_pairs={{0,64},{1,3},{2,66},{3,1},{4,68},{5,7},{6,70},{7,5},{8,72},{9,11},... | collective-permute-start | bytes 1966088 | tf_op jit(solution)/shard_map/ppermute | solution.py:48
  91.3 11.2 %collective-permute-start.7 = (f32[4,320,128]{2,1,0:T(8,128)S(1)}, f32[4,320,128]{2,1,0:T(8,128)S(1)}, u32[]{:S(2)}, u32[]{:S(2)}) collective-permute-start(f32[4,320,128]{2,1,0:T(8,128)S(1)} %pad_maximum_fusion.1.piece), channel_id=1, source_target_pairs={{0,192},{1,7},{2,194},{3,5},{4,196},{5,3},{6,198},{7,1},{8,200},{9... | collective-permute-start | bytes 1966088 | tf_op jit(solution)/shard_map/ppermute | solution.py:48
  103.8 8.1 %collective-permute-start.10 = (f32[2,320,384]{2,1,0:T(8,128)S(1)}, f32[2,320,384]{2,1,0:T(8,128)S(1)}, u32[]{:S(2)}, u32[]{:S(2)}) collective-permute-start(f32[2,320,384]{2,1,0:T(8,128)S(1)} %get-tuple-element.32.own), channel_id=1, source_target_pairs={{0,1},{1,0},{2,3},{3,2},{4,5},{5,4},{6,7},{7,6},{8,9},{9,8},{10,11... | collective-permute-start | bytes 2949128 | tf_op jit(solution)/shard_map/ppermute | solution.py:37
  109.7 16.6 %collective-permute-start.12 = (bf16[960,512]{1,0:T(8,128)(2,1)S(1)}, bf16[960,512]{1,0:T(8,128)(2,1)S(1)}, u32[]{:S(2)}, u32[]{:S(2)}) collective-permute-start(bf16[960,512]{1,0:T(8,128)(2,1)S(1)} %get-tuple-element.36.refs_1_), channel_id=1, source_target_pairs={{0,1},{1,0},{2,3},{3,2},{4,5},{5,4},{6,7},{7,6},{8,9},{9,8},{10,11... | collective-permute-start | bytes 2949128 | tf_op jit(solution)/shard_map/ppermute | solution.py:37
  109.8 16.5 %collective-permute-start.11 = (bf16[960,512]{1,0:T(8,128)(2,1)S(1)}, bf16[960,512]{1,0:T(8,128)(2,1)S(1)}, u32[]{:S(2)}, u32[]{:S(2)}) collective-permute-start(bf16[960,512]{1,0:T(8,128)(2,1)S(1)} %get-tuple-element.35.refs_0_), channel_id=1, source_target_pairs={{0,1},{1,0},{2,3},{3,2},{4,5},{5,4},{6,7},{7,6},{8,9},{9,8},{10,11... | collective-permute-start | bytes 2949128 | tf_op jit(solution)/shard_map/ppermute | solution.py:37
  110.2 16.1 %collective-permute-start.14 = (bf16[960,512]{1,0:T(8,128)(2,1)S(1)}, bf16[960,512]{1,0:T(8,128)(2,1)S(1)}, u32[]{:S(2)}, u32[]{:S(2)}) collective-permute-start(bf16[960,512]{1,0:T(8,128)(2,1)S(1)} %get-tuple-element.38.refs_3_), channel_id=1, source_target_pairs={{0,1},{1,0},{2,3},{3,2},{4,5},{5,4},{6,7},{7,6},{8,9},{9,8},{10,11... | collective-permute-start | bytes 2949128 | tf_op jit(solution)/shard_map/ppermute | solution.py:37
  110.3 16.0 %copy-start.2 = (bf16[512,4096]{1,0:T(8,128)(2,1)S(1)}, bf16[512,4096]{1,0:T(8,128)(2,1)}, u32[]{:S(2)}) copy-start(bf16[512,4096]{1,0:T(8,128)(2,1)} %features.3) | copy-start | bytes 12582916
  110.3 16.0 %collective-permute-start.13 = (bf16[960,512]{1,0:T(8,128)(2,1)S(1)}, bf16[960,512]{1,0:T(8,128)(2,1)S(1)}, u32[]{:S(2)}, u32[]{:S(2)}) collective-permute-start(bf16[960,512]{1,0:T(8,128)(2,1)S(1)} %get-tuple-element.37.refs_2_), channel_id=1, source_target_pairs={{0,1},{1,0},{2,3},{3,2},{4,5},{5,4},{6,7},{7,6},{8,9},{9,8},{10,11... | collective-permute-start | bytes 2949128 | tf_op jit(solution)/shard_map/ppermute | solution.py:37

commit v4 on v2

--- a/solution.py
+++ b/solution.py
@@ -18,6 +18,7 @@
 
 FIRST_AXIS = ("y", "x")
 SECOND_AXIS = ("x", "y")
+Z_AXIS = ("z", "z")
 STREAM_BITS = ((0, 1), (1, 0))
 
 
@@ -25,61 +26,72 @@
     return {"c": index & 1, "x": (index >> 1) & 3, "z": (index >> 3) & 7, "y": (index >> 6) & 3}
 
 
-def device_at(place):
-    return ((place["y"] * 8 + place["z"]) * 4 + place["x"]) * 2 + place["c"]
+def role_of(place):
+    return place["c"] ^ ((place["x"] + place["y"] + place["z"]) & 1)
 
 
 def gray(value):
     return value ^ (value >> 1)
 
 
+def gray_of(place, role, axes):
+    return jnp.where(role == 0, *(gray(place[axis]) for axis in axes))
+
+
 def across(block):
     return lax.ppermute(block, "rows", [(i, i ^ 1) for i in range(lax.axis_size("rows"))])
 
 
-def exchange(block, stream, step):
+def exchange(block, axes, bit):
     pairs = []
     for i in range(lax.axis_size("rows")):
         place = coordinates(i)
-        axis = FIRST_AXIS[place["c"]]
-        wanted = gray(place[axis]) ^ (1 << STREAM_BITS[stream][step])
-        place[axis] = next(v for v in range(4) if gray(v) == wanted)
-        pairs.append((i, device_at(place)))
+        role = role_of(place)
+        wanted = gray(place[axes[role]]) ^ (1 << bit)
+        place[axes[role]] = next(v for v in range(8) if gray(v) == wanted)
+        place["c"] ^= role ^ role_of(place)
+        there = ((place["y"] * 8 + place["z"]) * 4 + place["x"]) * 2 + place["c"]
+        pairs.append((i, there))
     return lax.ppermute(block, "rows", pairs)
 
 
-def all_to_all(block, axes):
-    size = block.shape[0]
-    groups = []
-    for i in range(lax.axis_size("rows")):
-        place = coordinates(i)
-        axis = axes[place["c"]]
-        if place[axis] == 0:
-            groups.append([device_at({**place, axis: k}) for k in range(size)])
-    return lax.all_to_all(block, "rows", 0, 0, axis_index_groups=groups, tiled=True)
-
-
-def scatter_sum(block, axes):
-    return jnp.sum(all_to_all(block, axes), axis=0)
-
-
-def gather(block, axes, size):
-    return all_to_all(jnp.broadcast_to(block[None], (size, *block.shape)), axes)
+def halve(block, place, axes, bit):
+    low, high = jnp.split(block, 2)
+    upper = (gray_of(place, role_of(place), axes) >> bit) & 1
+    sent = exchange(jnp.where(upper == 0, high, low), axes, bit)
+    return jnp.where(upper == 0, low, high) + sent
+
+
+def double(block, place, axes, bit):
+    upper = (gray_of(place, role_of(place), axes) >> bit) & 1
+    other = exchange(block, axes, bit)
+    return jnp.concatenate([jnp.where(upper == 0, block, other), jnp.where(upper == 0, other, block)])
+
+
+def inner_sum(block, place):
+    block = halve(block, place, SECOND_AXIS, 1)
+    block = halve(block, place, SECOND_AXIS, 0)[0]
+    block = halve(block, place, Z_AXIS, 0)
+    for bit in (1, 2):
+        block = block + exchange(block, Z_AXIS, bit)
+    block = double(block, place, Z_AXIS, 0)[None]
+    block = double(block, place, SECOND_AXIS, 0)
+    return double(block, place, SECOND_AXIS, 1)
 
 
 def order(place, half, stream):
-    core = place["c"] ^ half
-    code = jnp.where(core == 0, *(gray(place[axis]) for axis in FIRST_AXIS))
+    role = role_of(place) ^ half
+    code = gray_of(place, role, FIRST_AXIS)
     first, second = STREAM_BITS[stream]
-    return core, (((code >> first) & 1) << 2) | (((code >> second) & 1) << 1)
+    return role, (((code >> first) & 1) << 2) | (((code >> second) & 1) << 1)
 
 
 def cross_blocks(id_ref, features, sketches, outs):
     place = coordinates(id_ref[0])
     for (half, stream, start), out in outs:
-        core, mask = order(place, half, stream)
+        role, mask = order(place, half, stream)
         for pair in range(out.shape[0] // 2):
-            there = (core << 4) | (stream << 3) | ((start + 2 * pair) ^ mask)
+            there = (role << 4) | (stream << 3) | ((start + 2 * pair) ^ mask)
             columns = features[:, pl.ds(pl.multiple_of(there * LANES, 256), 256)]
             both = jnp.dot(sketches[...], columns, preferred_element_type=F32)
             cross = both[:SKETCH] + both[SKETCH:]
@@ -131,9 +143,10 @@
 
 
 def scatter_stream(stream, low, high, received):
-    back = exchange(high + received[4:], stream, 0)
+    first, second = STREAM_BITS[stream]
+    back = exchange(high + received[4:], FIRST_AXIS, first)
     block = low + received[:4]
-    back_next = exchange(block[2:] + back[2:], stream, 1)
+    back_next = exchange(block[2:] + back[2:], FIRST_AXIS, second)
     return block[:2] + back[:2] + back_next
 
 
@@ -278,8 +291,8 @@
 
 
 def columns_of(place, half, part, stream):
-    core, mask = order(place, half, stream)
-    first = (core << 4) | (stream << 3) | ((4 * part) ^ (mask & 4))
+    role, mask = order(place, half, stream)
+    first = (role << 4) | (stream << 3) | ((4 * part) ^ (mask & 4))
     return pl.ds(pl.multiple_of(first * LANES, WIDTH), WIDTH)
 
 
@@ -327,13 +340,12 @@
 
 
 def final_kernel(members, id_ref, features, basis_map, inverse_c, *refs):
-    terms, result = refs[:-1], refs[-1]
+    terms, (result, coeffs) = refs[:-2], refs[-2:]
     place = coordinates(id_ref[0])
-    total = jnp.zeros(result.shape, F32)
     for term, member in zip(terms, members):
-        coeffs = dot(basis_map[...], term[...])
-        total += dot_nt(coeffs.astype(BF16), features[:, columns_of(place, *member)])
-    result[...] = dot_three(inverse_c[...], total)
+        coeffs[:, columns_of(place, *member)] = dot(basis_map[...], term[...]).astype(BF16)
+    projected = dot_nt(coeffs[...], features[...])
+    result[...] = dot_three(inverse_c[...], projected)
 
 
 def body(features, sketch_matrix):
@@ -365,15 +377,12 @@
     block = jnp.concatenate(
         [scatter_stream(0, low0, high0, received[0]), scatter_stream(1, low1, high1, received[1])]
     )
-    block = scatter_sum(block, SECOND_AXIS)
-    block = scatter_sum(block.reshape(8, SKETCH // 8, LANES), ("z", "z"))
-    block = gather(block, ("z", "z"), 8).reshape(SKETCH, LANES)
-    block = gather(block, SECOND_AXIS, 4)
+    block = inner_sum(block, coordinates(device[0]))
     streams = []
-    for stream in range(2):
+    for stream, (first, second) in enumerate(STREAM_BITS):
         own = block[2 * stream : 2 * stream + 2]
-        own = jnp.concatenate([own, exchange(own, stream, 1)])
-        streams.append((own, exchange(own, stream, 0)))
+        own = jnp.concatenate([own, exchange(own, FIRST_AXIS, second)])
+        streams.append((own, exchange(own, FIRST_AXIS, first)))
 
     members = [(0, part, stream) for part in range(2) for stream in range(2)]
     terms_shape = ((3 * SKETCH, WIDTH), BF16)
@@ -407,6 +416,7 @@
         functools.partial(final_kernel, members),
         (device, features, basis_map, inverse_c, *terms),
         [((SKETCH, rows), F32)],
+        scratch=[pltpu.VMEM((SKETCH, width), BF16)],
         flops=4 * flops,
     )
     return result.T

time: 134 us -> 130 us (0.970)
  blocking collectives: 47.5 us -> 0 us
  waiting for transfers between devices: 33.3 us -> 67.5 us
  starting transfers between devices: 19.6 us -> 25.6 us
  other arithmetic: 0.71 us -> 4.09 us
    all_to_all x4 -> x0, blocking collectives: 47.5 us -> none  [all_to_all(): lax.all_to_all(block, 'rows', 0, 0, axis_index_groups=groups, tiled=True)]
    ppermute x8 -> x16, waiting for transfers between devices: 30.2 us -> 64.4 us  [exchange(): return lax.ppermute(block, 'rows', pairs)]
    ppermute x8 -> x16, starting transfers between devices: 5.1 us -> 21 us  [exchange(): return lax.ppermute(block, 'rows', pairs)]
    ppermute x7, starting transfers between devices: 14.5 us -> 4.63 us  [across(): lax.ppermute(block, 'rows', [(i, i ^ 1) for i in range(lax.axis_size('row...]
    add x4 -> x7, other arithmetic: 0.26 us -> 2.76 us  [the longest x2 1.51 us: scatter_stream(): back_next = exchange(block[2:] + back[2:], FIRST_AXIS, second)]
  transfers between devices with their start and end apart: 15 -> 23, of which waited for: 10 -> 18; matrix products, arithmetic and copies ran while one was open for 0% -> 1% of each run, Pallas kernels for 15% -> 15%
where the time goes in v4:
time: 130 us
  waiting for transfers between devices  67.5 us (52%)
  Pallas kernels  32.6 us (25%)
  starting transfers between devices  25.6 us (20%)
  other arithmetic  4.09 us (3%)
    ppermute x16, waiting for transfers between devices, exchange(): return lax.ppermute(block, 'rows', pairs)  64.4 us
    pallas_call x8, Pallas kernels, call(): pl.pallas_call(kernel, out_shape=[jax.ShapeDtypeStruct(shape, dtype) for...  32.6 us
    ppermute x16, starting transfers between devices, exchange(): return lax.ppermute(block, 'rows', pairs)  21 us
    ppermute x7, starting transfers between devices, across(): lax.ppermute(block, 'rows', [(i, i ^ 1) for i in range(lax.axis_size('row...  4.63 us
    ppermute x7, waiting for transfers between devices, across(): lax.ppermute(block, 'rows', [(i, i ^ 1) for i in range(lax.axis_size('row...  3.11 us
  transfers between devices with their start and end apart: 23, of which 18 were waited for; matrix products, arithmetic and copies ran while one was open for 1% of the time, Pallas kernels for 15%

profile of v4, /device:TPU:1, one launch (start us, length us, event | category | flops | bytes accessed | tf_op | source)
XLA Modules:
  0.0 130.0 jit_solution(9667481395642229232)
XLA Ops:
  0.0 5.3 %shard_map.28 = (bf16[640,512]{1,0:T(8,128)(2,1)S(1)}, f32[8,320,128]{2,1,0:T(8,128)S(1)}, f32[8,320,128]{2,1,0:T(8,128)S(1)}) custom-call(s32[1]{0:T(128)} %bitcast.id_ref, bf16[512,4096]{1,0:T(8,128)(2,1)} %features.3, bf16[320,4096]{1,0:T(8,128)(2,1)} %bitcast.13), custom_call_target="tpu_custom_call" | custom-call | flops 2684354560 | bytes 4194304 | tf_op jit(solution)/shard_map/pallas_call | solution.py:133
  5.3 3.3 %collective-permute-start.3 = (f32[8,320,128]{2,1,0:T(8,128)S(1)}, f32[8,320,128]{2,1,0:T(8,128)S(1)}, u32[]{:S(2)}, u32[]{:S(2)}) collective-permute-start(f32[8,320,128]{2,1,0:T(8,128)S(1)} %get-tuple-element.27), channel_id=1, source_target_pairs={{0,1},{1,0},{2,3},{3,2},{4,5},{5,4},{6,7},{7,6},{8,9},{9,8},{10,11... | collective-permute-start | bytes 3932168 | tf_op jit(solution)/shard_map/ppermute | solution.py:42
  8.8 1.5 %shard_map.29 = (f32[4,320,128]{2,1,0:T(8,128)S(1)}, f32[4,320,128]{2,1,0:T(8,128)S(1)}, f32[4,320,128]{2,1,0:T(8,128)S(1)}, f32[4,320,128]{2,1,0:T(8,128)S(1)}) custom-call(s32[1]{0:T(128)} %bitcast.id_ref, bf16[512,4096]{1,0:T(8,128)(2,1)S(1)} %copy-done.1, bf16[640,512]{1,0:T(8,128)(2,1)S(1)} %get-tuple-element.22.sketches), custom_call_target="tpu_custom_call" | custom-call | flops 1342177280 | bytes 4194304 | tf_op jit(solution)/shard_map/pallas_call | solution.py:133
  13.4 9.3 %collective-permute-done.4 = f32[4,320,128]{2,1,0:T(8,128)S(1)} collective-permute-done((f32[4,320,128]{2,1,0:T(8,128)S(1)}, f32[4,320,128]{2,1,0:T(8,128)S(1)}, u32[]{:S(2)}, u32[]{:S(2)}) %collective-permute-start.4) | collective-permute-done | bytes 655392 | tf_op jit(solution)/shard_map/ppermute | solution.py:55
  25.5 5.0 %collective-permute-done.5 = f32[2,320,128]{2,1,0:T(8,128)S(1)} collective-permute-done((f32[2,320,128]{2,1,0:T(8,128)}, f32[2,320,128]{2,1,0:T(8,128)S(1)}, u32[]{:S(2)}, u32[]{:S(2)}) %collective-permute-start.5) | collective-permute-done | bytes 327712 | tf_op jit(solution)/shard_map/ppermute | solution.py:55
  30.5 1.7 %collective-permute-done.2 = f32[2,320,128]{2,1,0:T(8,128)S(1)} collective-permute-done((f32[2,320,128]{2,1,0:T(8,128)}, f32[2,320,128]{2,1,0:T(8,128)S(1)}, u32[]{:S(2)}, u32[]{:S(2)}) %collective-permute-start.2) | collective-permute-done | bytes 327712 | tf_op jit(solution)/shard_map/ppermute | solution.py:55
  33.0 2.0 %collective-permute-start.6 = (f32[2,320,128]{2,1,0:T(8,128)}, f32[2,320,128]{2,1,0:T(8,128)}, u32[]{:S(2)}, u32[]{:S(2)}) collective-permute-start(f32[2,320,128]{2,1,0:T(8,128)} %broadcast_select_fusion.2), channel_id=1, source_target_pairs={{0,7},{1,192},{2,195},{3,4},{4,3},{5,196},{6,199},{7,0},{8,201},{9... | collective-permute-start | bytes 983048 | tf_op jit(solution)/shard_map/ppermute | solution.py:55
  35.1 6.0 %collective-permute-done.6 = f32[2,320,128]{2,1,0:T(8,128)} collective-permute-done((f32[2,320,128]{2,1,0:T(8,128)}, f32[2,320,128]{2,1,0:T(8,128)}, u32[]{:S(2)}, u32[]{:S(2)}) %collective-permute-start.6) | collective-permute-done | bytes 327712 | tf_op jit(solution)/shard_map/ppermute | solution.py:55
  42.4 4.7 %collective-permute-done.7 = f32[1,320,128]{2,1,0:T(8,128)S(1)} collective-permute-done((f32[1,320,128]{2,1,0:T(8,128)S(1)}, f32[1,320,128]{2,1,0:T(8,128)S(1)}, u32[]{:S(2)}, u32[]{:S(2)}) %collective-permute-start.7) | collective-permute-done | bytes 163872 | tf_op jit(solution)/shard_map/ppermute | solution.py:55
  48.2 3.5 %collective-permute-done.8 = f32[160,128]{1,0:T(8,128)S(1)} collective-permute-done((f32[160,128]{1,0:T(8,128)S(1)}, f32[160,128]{1,0:T(8,128)S(1)}, u32[]{:S(2)}, u32[]{:S(2)}) %collective-permute-start.8) | collective-permute-done | bytes 81952 | tf_op jit(solution)/shard_map/ppermute | solution.py:55
  51.7 3.3 %collective-permute-start.9 = (f32[160,128]{1,0:T(8,128)S(1)}, f32[160,128]{1,0:T(8,128)S(1)}, u32[]{:S(2)}, u32[]{:S(2)}) collective-permute-start(f32[160,128]{1,0:T(8,128)S(1)} %bitcast_add_fusion), channel_id=1, source_target_pairs={{0,25},{1,24},{2,27},{3,26},{4,29},{5,28},{6,31},{7,30},{8,17},{9,... | collective-permute-start | bytes 245768 | tf_op jit(solution)/shard_map/ppermute | solution.py:55
  55.0 3.1 %collective-permute-done.9 = f32[160,128]{1,0:T(8,128)S(1)} collective-permute-done((f32[160,128]{1,0:T(8,128)S(1)}, f32[160,128]{1,0:T(8,128)S(1)}, u32[]{:S(2)}, u32[]{:S(2)}) %collective-permute-start.9) | collective-permute-done | bytes 81952 | tf_op jit(solution)/shard_map/ppermute | solution.py:55
  58.1 4.2 %collective-permute-start.10 = (f32[160,128]{1,0:T(8,128)S(1)}, f32[160,128]{1,0:T(8,128)S(1)}, u32[]{:S(2)}, u32[]{:S(2)}) collective-permute-start(f32[160,128]{1,0:T(8,128)S(1)} %add.76), channel_id=1, source_target_pairs={{0,57},{1,56},{2,59},{3,58},{4,61},{5,60},{6,63},{7,62},{8,49},{9,... | collective-permute-start | bytes 245768 | tf_op jit(solution)/shard_map/ppermute | solution.py:55
  62.3 4.7 %collective-permute-done.10 = f32[160,128]{1,0:T(8,128)S(1)} collective-permute-done((f32[160,128]{1,0:T(8,128)S(1)}, f32[160,128]{1,0:T(8,128)S(1)}, u32[]{:S(2)}, u32[]{:S(2)}) %collective-permute-start.10) | collective-permute-done | bytes 81952 | tf_op jit(solution)/shard_map/ppermute | solution.py:55
  67.5 4.0 %collective-permute-done.11 = f32[160,128]{1,0:T(8,128)S(1)} collective-permute-done((f32[160,128]{1,0:T(8,128)S(1)}, f32[160,128]{1,0:T(8,128)S(1)}, u32[]{:S(2)}, u32[]{:S(2)}) %collective-permute-start.11) | collective-permute-done | bytes 81952 | tf_op jit(solution)/shard_map/ppermute | solution.py:55
  72.1 4.4 %collective-permute-done.12 = f32[1,320,128]{2,1,0:T(8,128)S(1)} collective-permute-done((f32[1,320,128]{2,1,0:T(8,128)S(1)}, f32[1,320,128]{2,1,0:T(8,128)S(1)}, u32[]{:S(2)}, u32[]{:S(2)}) %collective-permute-start.12) | collective-permute-done | bytes 163872 | tf_op jit(solution)/shard_map/ppermute | solution.py:55
  76.5 2.1 %collective-permute-start.13 = (f32[2,320,128]{2,1,0:T(8,128)S(1)}, f32[2,320,128]{2,1,0:T(8,128)S(1)}, u32[]{:S(2)}, u32[]{:S(2)}) collective-permute-start(f32[2,320,128]{2,1,0:T(8,128)S(1)} %pad_maximum_fusion.2), channel_id=1, source_target_pairs={{0,7},{1,192},{2,195},{3,4},{4,3},{5,196},{6,199},{7,0},{8,201},{9... | collective-permute-start | bytes 983048 | tf_op jit(solution)/shard_map/ppermute | solution.py:55
  78.6 5.7 %collective-permute-done.13 = f32[2,320,128]{2,1,0:T(8,128)S(1)} collective-permute-done((f32[2,320,128]{2,1,0:T(8,128)S(1)}, f32[2,320,128]{2,1,0:T(8,128)S(1)}, u32[]{:S(2)}, u32[]{:S(2)}) %collective-permute-start.13) | collective-permute-done | bytes 327712 | tf_op jit(solution)/shard_map/ppermute | solution.py:55
  84.3 3.3 %collective-permute-start.16 = (f32[2,320,128]{2,1,0:T(8,128)S(1)}, f32[2,320,128]{2,1,0:T(8,128)S(1)}, u32[]{:S(2)}, u32[]{:S(2)}) collective-permute-start(f32[2,320,128]{2,1,0:T(8,128)S(1)} %get-tuple-element.43), channel_id=1, source_target_pairs={{0,193},{1,6},{2,5},{3,194},{4,197},{5,2},{6,1},{7,198},{8,15},{9,... | collective-permute-start | bytes 983048 | tf_op jit(solution)/shard_map/ppermute | solution.py:55
  87.6 4.8 %collective-permute-done.16 = f32[2,320,128]{2,1,0:T(8,128)S(1)} collective-permute-done((f32[2,320,128]{2,1,0:T(8,128)S(1)}, f32[2,320,128]{2,1,0:T(8,128)S(1)}, u32[]{:S(2)}, u32[]{:S(2)}) %collective-permute-start.16) | collective-permute-done | bytes 327712 | tf_op jit(solution)/shard_map/ppermute | solution.py:55
  92.5 1.6 %collective-permute-done.14 = f32[2,320,128]{2,1,0:T(8,128)S(1)} collective-permute-done((f32[2,320,128]{2,1,0:T(8,128)S(1)}, f32[2,320,128]{2,1,0:T(8,128)S(1)}, u32[]{:S(2)}, u32[]{:S(2)}) %collective-permute-start.14) | collective-permute-done | bytes 327712 | tf_op jit(solution)/shard_map/ppermute | solution.py:55
  98.3 4.5 %collective-permute-done.17.piece = f32[4,320,128]{2,1,0:T(8,128)S(1)} collective-permute-done((f32[4,320,128]{2,1,0:T(8,128)S(1)}, f32[4,320,128]{2,1,0:T(8,128)S(1)}, u32[]{:S(2)}, u32[]{:S(2)}) %collective-permute-start.17) | collective-permute-done | bytes 655392 | tf_op jit(solution)/shard_map/ppermute | solution.py:55
  109.5 14.4 %shard_map.34 = (bf16[320,960]{1,0:T(8,128)(2,1)S(1)}, f32[320,320]{1,0:T(8,128)S(1)}) custom-call(s32[1]{0:T(128)} %bitcast.id_ref, f32[2,320,384]{2,1,0:T(8,128)S(1)} %get-tuple-element.32.own, f32[2,320,384]{2,1,0:T(8,128)S(1)} %collective-permute-done.18.other), custom_call_target="tpu_custom_call" | custom-call | flops 18790481920 | bytes 4194304 | tf_op jit(solution)/shard_map/pallas_call | solution.py:133
  123.9 6.1 %shard_map.35 = f32[320,512]{1,0:T(8,128)} custom-call(s32[1]{0:T(128)} %bitcast.id_ref, bf16[512,4096]{1,0:T(8,128)(2,1)S(1)} %copy-done.2, bf16[320,960]{1,0:T(8,128)(2,1)S(1)} %get-tuple-element.33.basis_map, f32[320,320]{1,0:T(8,128)S(1)} %get-tuple-element.34.inverse_c, bf16[960,512]{1,0:T(8,128)(2,1)S(1)} %get-tuple-element.35.refs_0_, ...), custom_call_target="tpu_custom_call" | custom-call | flops 5368709120 | bytes 4194304 | tf_op jit(solution)/shard_map/pallas_call | solution.py:133
  (57 shorter events, 21.2 us)
Async XLA Ops:
  5.3 6.0 %collective-permute-start.3 = (f32[8,320,128]{2,1,0:T(8,128)S(1)}, f32[8,320,128]{2,1,0:T(8,128)S(1)}, u32[]{:S(2)}, u32[]{:S(2)}) collective-permute-start(f32[8,320,128]{2,1,0:T(8,128)S(1)} %get-tuple-element.27), channel_id=1, source_target_pairs={{0,1},{1,0},{2,3},{3,2},{4,5},{5,4},{6,7},{7,6},{8,9},{9,8},{10,11... | collective-permute-start | bytes 3932168 | tf_op jit(solution)/shard_map/ppermute | solution.py:42
  8.7 4.5 %collective-permute-start = (f32[8,320,128]{2,1,0:T(8,128)S(1)}, f32[8,320,128]{2,1,0:T(8,128)S(1)}, u32[]{:S(2)}, u32[]{:S(2)}) collective-permute-start(f32[8,320,128]{2,1,0:T(8,128)S(1)} %get-tuple-element.24), channel_id=1, source_target_pairs={{0,1},{1,0},{2,3},{3,2},{4,5},{5,4},{6,7},{7,6},{8,9},{9,8},{10,11... | collective-permute-start | bytes 3932168 | tf_op jit(solution)/shard_map/ppermute | solution.py:42
  11.5 11.3 %collective-permute-start.4 = (f32[4,320,128]{2,1,0:T(8,128)S(1)}, f32[4,320,128]{2,1,0:T(8,128)S(1)}, u32[]{:S(2)}, u32[]{:S(2)}) collective-permute-start(f32[4,320,128]{2,1,0:T(8,128)S(1)} %get-tuple-element.40), channel_id=1, source_target_pairs={{0,193},{1,6},{2,5},{3,194},{4,197},{5,2},{6,1},{7,198},{8,15},{9,... | collective-permute-start | bytes 1966088 | tf_op jit(solution)/shard_map/ppermute | solution.py:55
  13.3 10.2 %collective-permute-start.1 = (f32[4,320,128]{2,1,0:T(8,128)S(1)}, f32[4,320,128]{2,1,0:T(8,128)S(1)}, u32[]{:S(2)}, u32[]{:S(2)}) collective-permute-start(f32[4,320,128]{2,1,0:T(8,128)S(1)} %get-tuple-element.42), channel_id=1, source_target_pairs={{0,65},{1,2},{2,1},{3,66},{4,69},{5,6},{6,5},{7,70},{8,11},{9,72},... | collective-permute-start | bytes 1966088 | tf_op jit(solution)/shard_map/ppermute | solution.py:55
  23.5 7.0 %collective-permute-start.5 = (f32[2,320,128]{2,1,0:T(8,128)}, f32[2,320,128]{2,1,0:T(8,128)S(1)}, u32[]{:S(2)}, u32[]{:S(2)}) collective-permute-start(f32[2,320,128]{2,1,0:T(8,128)} %slice_add_fusion.4), channel_id=1, source_target_pairs={{0,65},{1,2},{2,1},{3,66},{4,69},{5,6},{6,5},{7,70},{8,11},{9,72},... | collective-permute-start | bytes 983048 | tf_op jit(solution)/shard_map/ppermute | solution.py:55
  24.3 7.9 %collective-permute-start.2 = (f32[2,320,128]{2,1,0:T(8,128)}, f32[2,320,128]{2,1,0:T(8,128)S(1)}, u32[]{:S(2)}, u32[]{:S(2)}) collective-permute-start(f32[2,320,128]{2,1,0:T(8,128)} %slice_add_fusion.6), channel_id=1, source_target_pairs={{0,193},{1,6},{2,5},{3,194},{4,197},{5,2},{6,1},{7,198},{8,15},{9,... | collective-permute-start | bytes 983048 | tf_op jit(solution)/shard_map/ppermute | solution.py:55
  33.0 8.0 %collective-permute-start.6 = (f32[2,320,128]{2,1,0:T(8,128)}, f32[2,320,128]{2,1,0:T(8,128)}, u32[]{:S(2)}, u32[]{:S(2)}) collective-permute-start(f32[2,320,128]{2,1,0:T(8,128)} %broadcast_select_fusion.2), channel_id=1, source_target_pairs={{0,7},{1,192},{2,195},{3,4},{4,3},{5,196},{6,199},{7,0},{8,201},{9... | collective-permute-start | bytes 983048 | tf_op jit(solution)/shard_map/ppermute | solution.py:55
  42.3 4.8 %collective-permute-start.7 = (f32[1,320,128]{2,1,0:T(8,128)S(1)}, f32[1,320,128]{2,1,0:T(8,128)S(1)}, u32[]{:S(2)}, u32[]{:S(2)}) collective-permute-start(f32[1,320,128]{2,1,0:T(8,128)S(1)} %slice_select_fusion), channel_id=1, source_target_pairs={{0,3},{1,64},{2,67},{3,0},{4,7},{5,68},{6,71},{7,4},{8,73},{9,10},... | collective-permute-start | bytes 491528 | tf_op jit(solution)/shard_map/ppermute | solution.py:55
  47.2 4.5 %collective-permute-start.8 = (f32[160,128]{1,0:T(8,128)S(1)}, f32[160,128]{1,0:T(8,128)S(1)}, u32[]{:S(2)}, u32[]{:S(2)}) collective-permute-start(f32[160,128]{1,0:T(8,128)S(1)} %select_bitcast_fusion), channel_id=1, source_target_pairs={{0,9},{1,8},{2,11},{3,10},{4,13},{5,12},{6,15},{7,14},{8,1},{9,0},... | collective-permute-start | bytes 245768 | tf_op jit(solution)/shard_map/ppermute | solution.py:55
  51.7 6.4 %collective-permute-start.9 = (f32[160,128]{1,0:T(8,128)S(1)}, f32[160,128]{1,0:T(8,128)S(1)}, u32[]{:S(2)}, u32[]{:S(2)}) collective-permute-start(f32[160,128]{1,0:T(8,128)S(1)} %bitcast_add_fusion), channel_id=1, source_target_pairs={{0,25},{1,24},{2,27},{3,26},{4,29},{5,28},{6,31},{7,30},{8,17},{9,... | collective-permute-start | bytes 245768 | tf_op jit(solution)/shard_map/ppermute | solution.py:55
  58.1 8.9 %collective-permute-start.10 = (f32[160,128]{1,0:T(8,128)S(1)}, f32[160,128]{1,0:T(8,128)S(1)}, u32[]{:S(2)}, u32[]{:S(2)}) collective-permute-start(f32[160,128]{1,0:T(8,128)S(1)} %add.76), channel_id=1, source_target_pairs={{0,57},{1,56},{2,59},{3,58},{4,61},{5,60},{6,63},{7,62},{8,49},{9,... | collective-permute-start | bytes 245768 | tf_op jit(solution)/shard_map/ppermute | solution.py:55
  67.0 4.5 %collective-permute-start.11 = (f32[160,128]{1,0:T(8,128)S(1)}, f32[160,128]{1,0:T(8,128)S(1)}, u32[]{:S(2)}, u32[]{:S(2)}) collective-permute-start(f32[160,128]{1,0:T(8,128)S(1)} %add.77), channel_id=1, source_target_pairs={{0,9},{1,8},{2,11},{3,10},{4,13},{5,12},{6,15},{7,14},{8,1},{9,0},... | collective-permute-start | bytes 245768 | tf_op jit(solution)/shard_map/ppermute | solution.py:55
  71.6 4.8 %collective-permute-start.12 = (f32[1,320,128]{2,1,0:T(8,128)S(1)}, f32[1,320,128]{2,1,0:T(8,128)S(1)}, u32[]{:S(2)}, u32[]{:S(2)}) collective-permute-start(f32[1,320,128]{2,1,0:T(8,128)S(1)} %maximum_bitcast_fusion), channel_id=1, source_target_pairs={{0,3},{1,64},{2,67},{3,0},{4,7},{5,68},{6,71},{7,4},{8,73},{9,10},... | collective-permute-start | bytes 491528 | tf_op jit(solution)/shard_map/ppermute | solution.py:55
  76.5 7.8 %collective-permute-start.13 = (f32[2,320,128]{2,1,0:T(8,128)S(1)}, f32[2,320,128]{2,1,0:T(8,128)S(1)}, u32[]{:S(2)}, u32[]{:S(2)}) collective-permute-start(f32[2,320,128]{2,1,0:T(8,128)S(1)} %pad_maximum_fusion.2), channel_id=1, source_target_pairs={{0,7},{1,192},{2,195},{3,4},{4,3},{5,196},{6,199},{7,0},{8,201},{9... | collective-permute-start | bytes 983048 | tf_op jit(solution)/shard_map/ppermute | solution.py:55
  84.3 8.0 %collective-permute-start.16 = (f32[2,320,128]{2,1,0:T(8,128)S(1)}, f32[2,320,128]{2,1,0:T(8,128)S(1)}, u32[]{:S(2)}, u32[]{:S(2)}) collective-permute-start(f32[2,320,128]{2,1,0:T(8,128)S(1)} %get-tuple-element.43), channel_id=1, source_target_pairs={{0,193},{1,6},{2,5},{3,194},{4,197},{5,2},{6,1},{7,198},{8,15},{9,... | collective-permute-start | bytes 983048 | tf_op jit(solution)/shard_map/ppermute | solution.py:55
  87.6 6.5 %collective-permute-start.14 = (f32[2,320,128]{2,1,0:T(8,128)S(1)}, f32[2,320,128]{2,1,0:T(8,128)S(1)}, u32[]{:S(2)}, u32[]{:S(2)}) collective-permute-start(f32[2,320,128]{2,1,0:T(8,128)S(1)} %get-tuple-element.44), channel_id=1, source_target_pairs={{0,65},{1,2},{2,1},{3,66},{4,69},{5,6},{6,5},{7,70},{8,11},{9,72},... | collective-permute-start | bytes 983048 | tf_op jit(solution)/shard_map/ppermute | solution.py:55
  92.4 10.4 %collective-permute-start.17 = (f32[4,320,128]{2,1,0:T(8,128)S(1)}, f32[4,320,128]{2,1,0:T(8,128)S(1)}, u32[]{:S(2)}, u32[]{:S(2)}) collective-permute-start(f32[4,320,128]{2,1,0:T(8,128)S(1)} %pad_maximum_fusion.1.piece), channel_id=1, source_target_pairs={{0,65},{1,2},{2,1},{3,66},{4,69},{5,6},{6,5},{7,70},{8,11},{9,72},... | collective-permute-start | bytes 1966088 | tf_op jit(solution)/shard_map/ppermute | solution.py:55
  94.2 11.3 %collective-permute-start.15 = (f32[4,320,128]{2,1,0:T(8,128)S(1)}, f32[4,320,128]{2,1,0:T(8,128)S(1)}, u32[]{:S(2)}, u32[]{:S(2)}) collective-permute-start(f32[4,320,128]{2,1,0:T(8,128)S(1)} %pad_maximum_fusion.piece), channel_id=1, source_target_pairs={{0,193},{1,6},{2,5},{3,194},{4,197},{5,2},{6,1},{7,198},{8,15},{9,... | collective-permute-start | bytes 1966088 | tf_op jit(solution)/shard_map/ppermute | solution.py:55
  106.8 2.7 %collective-permute-start.18 = (f32[2,320,384]{2,1,0:T(8,128)S(1)}, f32[2,320,384]{2,1,0:T(8,128)S(1)}, u32[]{:S(2)}, u32[]{:S(2)}) collective-permute-start(f32[2,320,384]{2,1,0:T(8,128)S(1)} %get-tuple-element.32.own), channel_id=1, source_target_pairs={{0,1},{1,0},{2,3},{3,2},{4,5},{5,4},{6,7},{7,6},{8,9},{9,8},{10,11... | collective-permute-start | bytes 2949128 | tf_op jit(solution)/shard_map/ppermute | solution.py:42
  106.9 17.0 %collective-permute-start.20 = (bf16[960,512]{1,0:T(8,128)(2,1)S(1)}, bf16[960,512]{1,0:T(8,128)(2,1)S(1)}, u32[]{:S(2)}, u32[]{:S(2)}) collective-permute-start(bf16[960,512]{1,0:T(8,128)(2,1)S(1)} %get-tuple-element.36.refs_1_), channel_id=1, source_target_pairs={{0,1},{1,0},{2,3},{3,2},{4,5},{5,4},{6,7},{7,6},{8,9},{9,8},{10,11... | collective-permute-start | bytes 2949128 | tf_op jit(solution)/shard_map/ppermute | solution.py:42
  107.4 16.5 %collective-permute-start.19 = (bf16[960,512]{1,0:T(8,128)(2,1)S(1)}, bf16[960,512]{1,0:T(8,128)(2,1)S(1)}, u32[]{:S(2)}, u32[]{:S(2)}) collective-permute-start(bf16[960,512]{1,0:T(8,128)(2,1)S(1)} %get-tuple-element.35.refs_0_), channel_id=1, source_target_pairs={{0,1},{1,0},{2,3},{3,2},{4,5},{5,4},{6,7},{7,6},{8,9},{9,8},{10,11... | collective-permute-start | bytes 2949128 | tf_op jit(solution)/shard_map/ppermute | solution.py:42
  107.5 16.4 %collective-permute-start.22 = (bf16[960,512]{1,0:T(8,128)(2,1)S(1)}, bf16[960,512]{1,0:T(8,128)(2,1)S(1)}, u32[]{:S(2)}, u32[]{:S(2)}) collective-permute-start(bf16[960,512]{1,0:T(8,128)(2,1)S(1)} %get-tuple-element.38.refs_3_), channel_id=1, source_target_pairs={{0,1},{1,0},{2,3},{3,2},{4,5},{5,4},{6,7},{7,6},{8,9},{9,8},{10,11... | collective-permute-start | bytes 2949128 | tf_op jit(solution)/shard_map/ppermute | solution.py:42
  107.9 16.0 %copy-start.2 = (bf16[512,4096]{1,0:T(8,128)(2,1)S(1)}, bf16[512,4096]{1,0:T(8,128)(2,1)}, u32[]{:S(2)}) copy-start(bf16[512,4096]{1,0:T(8,128)(2,1)} %features.3) | copy-start | bytes 12582916
  107.9 16.0 %collective-permute-start.21 = (bf16[960,512]{1,0:T(8,128)(2,1)S(1)}, bf16[960,512]{1,0:T(8,128)(2,1)S(1)}, u32[]{:S(2)}, u32[]{:S(2)}) collective-permute-start(bf16[960,512]{1,0:T(8,128)(2,1)S(1)} %get-tuple-element.37.refs_2_), channel_id=1, source_target_pairs={{0,1},{1,0},{2,3},{3,2},{4,5},{5,4},{6,7},{7,6},{8,9},{9,8},{10,11... | collective-permute-start | bytes 2949128 | tf_op jit(solution)/shard_map/ppermute | solution.py:42
  (3 other events, 19.6 us)
